TPU v7x, 256 devices: a whole 4x4x8 slice. The times are simulated.
256 devices in a mesh: dp: 32 (over z, y), shard: 8 (over x, core).
Axes of the slice: x: 4, y: 4, z: 8, core: 2. Of those that a mesh axis runs over, the one named last changes fastest.
Arguments:
- gradient: bfloat16 [32, 3072, 3968], P('dp', 'shard'), may hold values from -6 to 6
- memory: bfloat16 [32, 3072, 3968], P('dp', 'shard'), may hold values from -4 to 4
- old_factor: bfloat16 [3968, 128], replicated, may hold values from -0.09375 to 0.09375
Outputs:
- new_memory: bfloat16 [32, 3072, 3968], P('dp', 'shard')
- new_factor: float32 [3968, 128], replicated
All inputs are finite; a program needn't handle non-finite values.
Results may differ from a plain program's by a relative error of at most 0.001.
Values sent between devices are 32-bit elements; how exact they have to be, the bound alone decides.
A program may use at most 64 MiB of HBM per device.

v0:
```python
import jax
import jax.numpy as jnp
from jax import lax
from jax.sharding import PartitionSpec as P


def per_device(gradient, memory, old_factor):
    replicas = lax.axis_size("dp")
    corrected = gradient[0].astype(jnp.float32) + memory[0].astype(jnp.float32)
    factor = old_factor.astype(jnp.float32)
    local_span = jnp.dot(corrected, factor, precision=lax.Precision.HIGHEST)
    spanned = lax.psum(local_span, "dp") / replicas
    local_gram = jnp.dot(spanned.T, spanned, precision=lax.Precision.HIGHEST)
    gram_matrix = lax.psum(local_gram, "shard")
    lower_factor = jnp.linalg.cholesky(gram_matrix)
    orthonormal = jax.scipy.linalg.solve_triangular(lower_factor, spanned.T, lower=True).T
    local_term = jnp.einsum("hd,hk->dk", corrected, orthonormal, precision=lax.Precision.HIGHEST)
    new_factor = lax.psum(local_term, ("dp", "shard")) / replicas
    decompressed = jnp.dot(orthonormal, new_factor.T, precision=lax.Precision.HIGHEST)
    new_memory = (corrected - decompressed).astype(jnp.bfloat16)[None]
    return (new_memory, new_factor)


def solution(mesh):
    in_specs = (P("dp", "shard", None), P("dp", "shard", None), P())
    out_specs = (P("dp", "shard", None), P())
    return jax.shard_map(
        per_device, mesh=mesh, in_specs=in_specs, out_specs=out_specs, check_vma=False
    )
```

profile of v0, /device:TPU:1, one launch (start us, length us, event | category | flops | bytes accessed | tf_op | source)
XLA Modules:
  0.0 542.4 jit_solution(7879976745934933043)
XLA Ops:
  7.2 0.0 copy-start
  7.2 0.0 all-reduce.4.cloned.1.call-start
  7.2 1.2 copy-done
  8.4 6.6 %fusion.2 = f32[384,128]{1,0:T(8,128)} fusion(bf16[3968,128]{1,0:T(8,128)(2,1)S(1)} %copy-done, bf16[1,384,3968]{2,1,0:T(8,128)(2,1)} %param.4, bf16[1,384,3968]{2,1,0:T(8,128)(2,1)} %param.3), kind=kOutput, calls=%fused_computation.3 | convolution fusion | flops 2344992768 | bytes 7307264 | tf_op jit(solution)/shard_map/dot_general | solution.py:11
  14.9 0.0 all-reduce.4.cloned.1.call-update
  15.0 0.0 all-reduce.6.cloned.1.call-start
  15.0 142.0 %all-reduce.4.cloned.1.call-done = f32[384,128]{1,0:T(8,128)} async-done(((f32[384,128]{1,0:T(8,128)}), f32[384,128]{1,0:T(8,128)}) %all-reduce.4.cloned.1.call-update) | async-done | bytes 196624 | tf_op jit(solution)/shard_map/psum | solution.py:12
  157.1 2.1 fusion.8
  159.2 0.0 all-reduce.6.cloned.1.call-update
  159.2 0.0 all-reduce.8.cloned.1.call-start
  159.3 64.4 %all-reduce.6.cloned.1.call-done = f32[128,128]{0,1:T(8,128)} async-done(((f32[128,128]{0,1:T(8,128)}), f32[128,128]{0,1:T(8,128)}) %all-reduce.6.cloned.1.call-update) | async-done | bytes 65552 | tf_op jit(solution)/shard_map/psum | solution.py:14
  223.7 0.9 copy.6
  224.6 0.9 fusion.14
  225.5 11.7 %cholesky.16 = f32[128,128]{1,0:T(8,128)S(1)} custom-call(f32[128,128]{1,0:T(8,128)S(1)} %fusion.14), custom_call_target="Cholesky" | custom-call | tf_op jit(solution)/shard_map/jit(cholesky)/cholesky | solution.py:15
  237.2 0.6 compare_reduce_fusion
  237.9 0.7 fusion.12
  238.5 9.8 %custom-call.7 = f32[1,128,128]{1,2,0:T(8,128)S(1)} custom-call(f32[1,128,128]{2,1,0:T(8,128)S(1)} %fusion.12), custom_call_target="InvertDiagBlocksLowerTriangular" | custom-call | tf_op jit(solution)/shard_map/jit(_solve_triangular)/triangular_solve | solution.py:16
  248.4 1.3 fusion.6
  249.7 13.4 %fusion = f32[3968,128]{1,0:T(8,128)} fusion(f32[128,384]{1,0:T(8,128)S(1)} %fusion.6, bf16[1,384,3968]{2,1,0:T(8,128)(2,1)} %param.4, bf16[1,384,3968]{2,1,0:T(8,128)(2,1)} %param.3), kind=kOutput, calls=%fused_computation.1 | convolution fusion | flops 2344992768 | bytes 8323072 | tf_op jit(solution)/shard_map/hd,hk->dk/dot_general | solution.py:17
  263.1 0.0 all-reduce.8.cloned.1.call-update
  263.1 261.0 %all-reduce.8.cloned.1.call-done = f32[3968,128]{1,0:T(8,128)} async-done(((f32[3968,128]{1,0:T(8,128)}), f32[3968,128]{1,0:T(8,128)}) %all-reduce.8.cloned.1.call-update) | async-done | bytes 2031632 | tf_op jit(solution)/shard_map/psum | solution.py:18
  524.1 1.8 broadcast_multiply_fusion
  526.0 0.6 copy-done.1
  526.6 9.3 %fusion.5 = bf16[1,384,3968]{2,1,0:T(8,128)(2,1)} fusion(f32[128,384]{1,0:T(8,128)S(1)} %fusion.6, f32[3968,128]{1,0:T(8,128)S(1)} %broadcast_multiply_fusion, bf16[1,384,3968]{2,1,0:T(8,128)(2,1)S(1)} %copy-done.1, bf16[1,384,3968]{2,1,0:T(8,128)(2,1)} %param.3), kind=kOutput, calls=%fused_computation.7 | convolution fusion | flops 2348040192 | bytes 11370496 | tf_op jit(solution)/shard_map/dot_general | solution.py:19
  (4 shorter events, 0.0 us)
Async XLA Ops:
  7.2 1.2 copy-start
  7.2 149.9 %all-reduce.4.cloned.1.call-start = ((), (), s32[]{:S(2)}) async-start(), calls=%async_computation | async-start | bytes 393216 | tf_op jit(solution)/shard_map/psum | solution.py:12
  15.0 208.7 %all-reduce.6.cloned.1.call-start = ((), (), s32[]{:S(2)}) async-start(), calls=%async_computation.1 | async-start | bytes 131072 | tf_op jit(solution)/shard_map/psum | solution.py:14
  159.2 364.9 %all-reduce.8.cloned.1.call-start = ((), (), s32[]{:S(2)}) async-start(), calls=%async_computation.2 | async-start | bytes 4063232 | tf_op jit(solution)/shard_map/psum | solution.py:18
  524.1 2.5 copy-start.1
  526.6 9.3 %copy-start.2 = (f32[3968,128]{1,0:T(8,128)}, f32[3968,128]{1,0:T(8,128)S(1)}, u32[]{:S(2)}) copy-start(f32[3968,128]{1,0:T(8,128)S(1)} %broadcast_multiply_fusion) | copy-start | bytes 6094852
Sparse Core Ops, SparseCore 0:
  15.1 141.9 all-reduce.3
  160.0 63.6 all-reduce.5
  263.2 260.8 all-reduce.7
where the time goes:
time: 543 us; the launch traced here: 542 us
  waiting for transfers between devices  468 us (86%)
  matrix products  32.7 us (6%)
  other arithmetic  25.6 us (5%)
  between operations  13.8 us (3%)
    psum x1, waiting for transfers between devices, per_device(): new_factor = lax.psum(local_term, ('dp', 'shard')) / replicas  261 us
    psum x1, waiting for transfers between devices, per_device(): spanned = lax.psum(local_span, 'dp') / replicas  142 us
    psum x1, waiting for transfers between devices, per_device(): gram_matrix = lax.psum(local_gram, 'shard')  64.4 us
    dot_general x1, matrix products, per_device(): jnp.einsum('hd,hk->dk', corrected, orthonormal, precision=lax.Precision.H...  13.4 us
    another operation x3, other arithmetic, per_device(): lower_factor = jnp.linalg.cholesky(gram_matrix)  12.4 us
  transfers between devices with their start and end apart: 3, of which 3 were waited for; matrix products, arithmetic and copies ran while one was open for 0% of the time, Pallas kernels for 0%

commit v1 on v0

v1 whole, which is shorter than its diff:
```python
import functools

import jax
import jax.numpy as jnp
from jax import lax
from jax.experimental import pallas as pl
from jax.experimental.pallas import tpu as pltpu
from jax.sharding import PartitionSpec as P

MESH = pl.DeviceIdType.MESH
D = 3968
RANK = 128
ROWS = 384
ZS, YS, XS, CORES = 8, 4, 4, 2
DP = ZS * YS
PIECE = ROWS // DP
PADDED = 4096
HALF = PADDED // CORES
BIG = HALF // 4
MID = BIG // 4
SMALL = MID // ZS
BLOCKS = D // 128
ORDER = (2, 1, 3, 0)
VMEM_BYTES = 48 * 1024 * 1024


def eight_columns(step, gram, inverse):
    row = lax.broadcasted_iota(jnp.int32, (RANK, 1), 0)
    row8 = lax.broadcasted_iota(jnp.int32, (8, RANK), 0)
    live = row[8:] + 8 * step < RANK
    columns = [jnp.broadcast_to(gram[:, k:k + 1], (RANK, RANK)) for k in range(8)]
    top = [column[:8] for column in columns]
    below = [jnp.where(live, column[8:], 0.0) for column in columns]
    gram8, inverse8 = gram[:8], inverse[:8]
    gram_rest, inverse_rest = gram[8:], inverse[8:]
    pivots = []
    for k in range(8):
        pivot = jnp.broadcast_to(top[k][k:k + 1], (8, RANK))
        reciprocal = 1.0 / pivot
        pivots.append(pivot[:1])
        factor8 = jnp.where(row8 > k, top[k] * reciprocal, 0.0)
        factor = below[k] * reciprocal[:1]
        for j in range(k + 1, 8):
            upper = top[j][k:k + 1]
            top[j] = top[j] - factor8 * upper
            below[j] = below[j] - factor * upper
        gram_row, inverse_row = gram8[k:k + 1], inverse8[k:k + 1]
        gram_rest = gram_rest - factor * gram_row
        inverse_rest = inverse_rest - factor * inverse_row
        gram8 = gram8 - factor8 * gram_row
        inverse8 = inverse8 - factor8 * inverse_row
    done = inverse8 * lax.rsqrt(jnp.concatenate(pivots, 0))
    inverse = jnp.concatenate([inverse_rest, done], 0)
    gram = jnp.concatenate([gram_rest, gram8], 0)
    return pltpu.roll(gram, RANK - 8, 1), inverse


def split(value):
    high = value.astype(jnp.bfloat16)
    return high, (value - high.astype(jnp.float32)).astype(jnp.bfloat16)


def land(ref, sem):
    pltpu.make_async_copy(ref, ref, sem).wait()


def exchange_kernel(g_hbm, m_hbm, f_hbm, n_ref, o_ref,
                    g, m, f, gt, mt, part, part_in, span_all, span, span2,
                    gram, gram_in, gram_x, gram_back, lower, inverse, x, core_in, a_in, b_in, z_in,
                    load_sem, part_send, part_recv, span_send, span_recv,
                    gram_send, gram_recv, core_send, core_recv, a_send, a_recv, b_send, b_recv,
                    z_send, z_recv, gz_send, gz_recv, gb_send, gb_recv, ga_send, ga_recv, gc_send, gc_recv):
    dp, shard = lax.axis_index("dp"), lax.axis_index("shard")
    zi, yi = dp // YS, dp % YS
    xi, ci = shard // CORES, shard % CORES
    a = xi * (1 - ci) + yi * ci
    b = yi * (1 - ci) + xi * ci

    def plane_peer(j):
        return (j, shard)

    def a_peer(k):
        return (zi * YS + (yi + k * ci) % 4, ((xi + k * (1 - ci)) % 4) * CORES + ci)

    def b_peer(k):
        return (zi * YS + (yi + k * (1 - ci)) % 4, ((xi + k * ci) % 4) * CORES + ci)

    def x_peer(k):
        return (dp, ((xi + k) % 4) * CORES + ci)

    def z_peer(k):
        return (((zi + k) % ZS) * YS + yi, shard)

    sibling = (dp, xi * CORES + 1 - ci)

    def send(src, dst, send_sem, recv_sem, to):
        pltpu.make_async_remote_copy(src_ref=src, dst_ref=dst, send_sem=send_sem, recv_sem=recv_sem,
                                     device_id=to, device_id_type=MESH).start()

    load_f = pltpu.make_async_copy(f_hbm, f, load_sem.at[8])
    load_f.start()

    def part_rows(i):
        q = (zi // 2 + 6 - i) % 4
        return q, pl.ds(pl.multiple_of(q * 96, 96), 96)

    def loads(i):
        _, rows = part_rows(i)
        return (pltpu.make_async_copy(g_hbm.at[rows], g.at[rows], load_sem.at[2 * i]),
                pltpu.make_async_copy(m_hbm.at[rows], m.at[rows], load_sem.at[2 * i + 1]))

    for i in range(4):
        for copy in loads(i):
            copy.start()

    barrier = pltpu.get_barrier_semaphore()

    def greet(k, _):
        pl.semaphore_signal(barrier, inc=1, device_id=plane_peer((dp + k) % DP), device_id_type=MESH)
        return 0
    lax.fori_loop(1, DP, greet, 0)
    for k in (1, 2, 3):
        pl.semaphore_signal(barrier, inc=1, device_id=x_peer(k), device_id_type=MESH)
    pl.semaphore_signal(barrier, inc=1, device_id=sibling, device_id_type=MESH)

    load_f.wait()
    for i in range(4):
        q, rows = part_rows(i)
        for copy in loads(i):
            copy.wait()
        value = (jnp.dot(g[rows, :], f[...], preferred_element_type=jnp.float32)
                 + jnp.dot(m[rows, :], f[...], preferred_element_type=jnp.float32))
        for j in range(8):
            part[q * 8 + j] = value[PIECE * j:PIECE * (j + 1)]
        if i == 0:
            pl.semaphore_wait(barrier, DP + 3)

        def scatter(j, _):
            to = q * 8 + j

            @pl.when(to != dp)
            def _():
                send(part.at[to], part_in.at[(to - dp + DP) % DP - 1], part_send, part_recv, plane_peer(to))
            return 0
        lax.fori_loop(0, 8, scatter, 0)

    def turn(i, _):
        lanes = pl.ds(pl.multiple_of(i * 128, 128), 128)
        gt[lanes, :] = g[:, lanes].T
        mt[lanes, :] = m[:, lanes].T
        return 0
    lax.fori_loop(0, BLOCKS, turn, 0)
    gt[D:, :] = jnp.zeros((PADDED - D, ROWS), jnp.bfloat16)
    mt[D:, :] = jnp.zeros((PADDED - D, ROWS), jnp.bfloat16)

    land(part_in, part_recv)
    total = part[dp]
    for k in range(DP - 1):
        total = total + part_in[k]
    span_all[dp] = total * (1.0 / DP)

    def spread(k, _):
        send(span_all.at[dp], span_all.at[dp], span_send, span_recv, plane_peer((dp + k) % DP))
        return 0
    lax.fori_loop(1, DP, spread, 0)
    land(span_all.at[pl.ds(0, DP - 1)], span_recv)

    for j in range(DP // 2):
        span[24 * j:24 * (j + 1), :] = jnp.concatenate([span_all[2 * j], span_all[2 * j + 1]], 0)
    high, low = split(span[...])
    span2[:, :RANK] = high
    span2[:, RANK:] = low

    gram[...] = lax.dot_general(span[...], span[...], (((0,), (0,)), ((), ())),
                                precision=lax.Precision.HIGHEST, preferred_element_type=jnp.float32)
    mine = pl.ds(pl.multiple_of(ci * 64, 64), 64)
    other = pl.ds(pl.multiple_of((1 - ci) * 64, 64), 64)
    send(gram.at[other], gram_in, gram_send.at[0], gram_recv.at[0], sibling)

    def product(start):
        rows = pl.ds(start, BIG)
        both = (jnp.dot(gt[rows, :], span2[...], preferred_element_type=jnp.float32)
                + jnp.dot(mt[rows, :], span2[...], preferred_element_type=jnp.float32))
        return both[:, :RANK] + both[:, RANK:]

    for i, k in enumerate(ORDER):
        start = pl.multiple_of((1 - ci) * HALF + ((b + k) % 4) * BIG, BIG)
        x[pl.ds(start, BIG), :] = product(start)
        send(x.at[pl.ds(start, BIG)], core_in.at[i], core_send, core_recv.at[i], sibling)
        if i == 0:
            land(gram_in, gram_recv.at[0])
            gram[mine, :] = gram[mine, :] + gram_in[...]
            for r in (1, 2, 3):
                send(gram.at[mine], gram_x.at[r - 1], gram_send.at[1], gram_recv.at[1], x_peer(r))

    for i, k in enumerate(ORDER):
        start = pl.multiple_of(ci * HALF + ((a + k) % 4) * BIG, BIG)
        value = product(start)
        land(core_in.at[i], core_recv.at[i])
        x[pl.ds(start, BIG), :] = value + core_in[i]
        if k:
            for j, kb in enumerate(ORDER):
                rows = pl.ds(pl.multiple_of(start + ((b + kb) % 4) * MID, MID), MID)
                send(x.at[rows], a_in.at[i, j], a_send, a_recv.at[i, j], a_peer(k))

    land(gram_x, gram_recv.at[1])
    land(gram_x, gram_send.at[1])
    gram[mine, :] = gram[mine, :] + gram_x[0] + gram_x[1] + gram_x[2]
    land(gram_in, gram_send.at[0])
    send(gram.at[mine], gram_back, gram_send.at[2], gram_recv.at[2], sibling)
    land(gram_back, gram_recv.at[2])
    lower[mine, :] = gram[mine, :]
    lower[other, :] = gram_back[...]
    row = lax.broadcasted_iota(jnp.int32, (RANK, RANK), 0)
    lane = lax.broadcasted_iota(jnp.int32, (RANK, RANK), 1)
    inverse[...] = (row == lane).astype(jnp.float32)

    def eliminate(first, last):
        def one(step, _):
            lower[...], inverse[...] = eight_columns(step, lower[...], inverse[...])
            return 0
        lax.fori_loop(first, last, one, 0)

    own = pl.multiple_of(ci * HALF + a * BIG, BIG)
    for j, kb in enumerate(ORDER):
        eliminate(2 * j, 2 * j + 2)
        rows = pl.ds(pl.multiple_of(own + ((b + kb) % 4) * MID, MID), MID)
        for i in range(3):
            land(a_in.at[i, j], a_recv.at[i, j])
        x[rows, :] = x[rows, :] + a_in[0, j] + a_in[1, j] + a_in[2, j]
        if kb:
            send(x.at[rows], b_in.at[j], b_send, b_recv.at[j], b_peer(kb))
    eliminate(8, 10)
    block = pl.multiple_of(own + b * MID, MID)
    rows = pl.ds(block, MID)
    for j in range(3):
        land(b_in.at[j], b_recv.at[j])
    x[rows, :] = x[rows, :] + b_in[0] + b_in[1] + b_in[2]
    for k in range(1, ZS):
        target = pl.ds(pl.multiple_of(block + ((zi + k) % ZS) * SMALL, SMALL), SMALL)
        send(x.at[target], z_in.at[k - 1], z_send, z_recv, z_peer(k))
    eliminate(10, 16)
    last = pl.ds(pl.multiple_of(block + zi * SMALL, SMALL), SMALL)
    land(z_in, z_recv)
    total = x[last, :]
    for k in range(ZS - 1):
        total = total + z_in[k]

    n_ref[last, :] = lax.dot_general(total * (1.0 / DP), inverse[...], (((1,), (1,)), ((), ())),
                                     precision=lax.Precision.HIGHEST, preferred_element_type=jnp.float32)
    for k in range(1, ZS):
        send(n_ref.at[last], n_ref.at[last], gz_send, gz_recv, z_peer(k))
    o_ref[...] = lax.dot_general(span[...], inverse[...], (((1,), (1,)), ((), ())),
                                 precision=lax.Precision.HIGHEST, preferred_element_type=jnp.float32)
    land(n_ref.at[pl.ds(0, (ZS - 1) * SMALL)], gz_recv)
    for j, kb in enumerate(ORDER[:3]):
        send(n_ref.at[rows], n_ref.at[rows], gb_send, gb_recv.at[j], b_peer(kb))
    for j, kb in enumerate((0, 2, 1, 3)):
        here = pl.ds(pl.multiple_of(own + ((b - kb + 4) % 4) * MID, MID), MID)
        if kb:
            land(n_ref.at[here], gb_recv.at[ORDER.index(kb)])
        for i, k in enumerate(ORDER[:3]):
            send(n_ref.at[here], n_ref.at[here], ga_send, ga_recv.at[i, j], a_peer(k))
        send(n_ref.at[here], n_ref.at[here], gc_send, gc_recv.at[0, j], sibling)
    for j, kb in enumerate((0, 2, 1, 3)):
        for i, k in enumerate(ORDER[:3]):
            there = pl.ds(pl.multiple_of(ci * HALF + ((a - k + 4) % 4) * BIG + ((b - kb + 4) % 4) * MID, MID), MID)
            land(n_ref.at[there], ga_recv.at[i, j])
            send(n_ref.at[there], n_ref.at[there], gc_send, gc_recv.at[i + 1, j], sibling)
    for i in range(4):
        for j in range(4):
            land(n_ref.at[pl.ds(0, MID)], gc_recv.at[i, j])

    land(part_in, part_send)
    land(part_in, span_send)
    land(gram_in, gram_send.at[2])
    land(x.at[pl.ds(0, HALF)], core_send)
    land(a_in, a_send)
    land(b_in, b_send)
    land(z_in, z_send)
    land(z_in, gz_send)
    land(b_in, gb_send)
    land(a_in, ga_send)
    land(x.at[pl.ds(0, HALF)], gc_send)


def exchange(g, m, f):
    dma = pltpu.SemaphoreType.DMA
    f32, bf16 = jnp.float32, jnp.bfloat16
    return pl.pallas_call(
        exchange_kernel,
        out_shape=(jax.ShapeDtypeStruct((PADDED, RANK), f32), jax.ShapeDtypeStruct((ROWS, RANK), f32)),
        in_specs=[pl.BlockSpec(memory_space=pl.ANY)] * 3,
        out_specs=(pl.BlockSpec(memory_space=pltpu.VMEM), pl.BlockSpec(memory_space=pltpu.VMEM)),
        scratch_shapes=[
            pltpu.VMEM((ROWS, D), bf16), pltpu.VMEM((ROWS, D), bf16), pltpu.VMEM((D, RANK), bf16),
            pltpu.VMEM((PADDED, ROWS), bf16), pltpu.VMEM((PADDED, ROWS), bf16),
            pltpu.VMEM((DP, PIECE, RANK), f32), pltpu.VMEM((DP - 1, PIECE, RANK), f32),
            pltpu.VMEM((DP, PIECE, RANK), f32), pltpu.VMEM((ROWS, RANK), f32), pltpu.VMEM((ROWS, 2 * RANK), bf16),
            pltpu.VMEM((RANK, RANK), f32), pltpu.VMEM((64, RANK), f32), pltpu.VMEM((3, 64, RANK), f32),
            pltpu.VMEM((64, RANK), f32),
            pltpu.VMEM((RANK, RANK), f32), pltpu.VMEM((RANK, RANK), f32),
            pltpu.VMEM((PADDED, RANK), f32), pltpu.VMEM((4, BIG, RANK), f32),
            pltpu.VMEM((3, 4, MID, RANK), f32), pltpu.VMEM((3, MID, RANK), f32),
            pltpu.VMEM((ZS - 1, SMALL, RANK), f32),
            dma((9,)), dma, dma, dma, dma, dma((3,)), dma((3,)), dma, dma((4,)), dma, dma((3, 4)), dma, dma((3,)),
            dma, dma, dma, dma, dma, dma((3,)), dma, dma((3, 4)), dma, dma((4, 4)),
        ],
        compiler_params=pltpu.CompilerParams(collective_id=0, has_side_effects=True, vmem_limit_bytes=VMEM_BYTES),
        cost_estimate=pl.CostEstimate(flops=4 * 10 ** 9, bytes_accessed=10 ** 7, transcendentals=0),
        name="exchange",
    )(g, m, f)


def residual_kernel(g_ref, m_ref, o_ref, n_ref, memory_ref, factor_ref, n_high, n_low):
    step = pl.program_id(0)

    @pl.when(step == 0)
    def _():
        high, low = split(n_ref[...])
        n_high[...] = high
        n_low[...] = low

    high, low = split(o_ref[...])

    def times(left, right):
        return lax.dot_general(left, right, (((1,), (1,)), ((), ())), preferred_element_type=jnp.float32)

    for start in range(0, D, 512):
        size = min(512, D - start)
        cols = pl.ds(start, size)
        update = (times(high, n_high[cols, :]) + times(high, n_low[cols, :])) + times(low, n_high[cols, :])
        corrected = g_ref[:, cols].astype(jnp.float32) + m_ref[:, cols].astype(jnp.float32)
        memory_ref[:, cols] = (corrected - update).astype(jnp.bfloat16)
    quarter = D // 4
    factor_ref[...] = n_ref[pl.ds(pl.multiple_of(step * quarter, quarter), quarter), :]


def residual(g, m, o, n):
    rows = ROWS // 4
    return pl.pallas_call(
        residual_kernel,
        grid=(4,),
        out_shape=(jax.ShapeDtypeStruct((ROWS, D), jnp.bfloat16), jax.ShapeDtypeStruct((D, RANK), jnp.float32)),
        in_specs=[
            pl.BlockSpec((rows, D), lambda i: (i, 0)), pl.BlockSpec((rows, D), lambda i: (i, 0)),
            pl.BlockSpec((rows, RANK), lambda i: (i, 0)), pl.BlockSpec((PADDED, RANK), lambda i: (0, 0)),
        ],
        out_specs=(pl.BlockSpec((rows, D), lambda i: (i, 0)), pl.BlockSpec((D // 4, RANK), lambda i: (i, 0))),
        scratch_shapes=[pltpu.VMEM((PADDED, RANK), jnp.bfloat16), pltpu.VMEM((PADDED, RANK), jnp.bfloat16)],
        compiler_params=pltpu.CompilerParams(vmem_limit_bytes=VMEM_BYTES),
        name="residual",
    )(g, m, o, n)


def per_device(gradient, memory, old_factor):
    g, m = gradient[0], memory[0]
    n, o = exchange(g, m, old_factor)
    new_memory, new_factor = residual(g, m, o, n)
    return (new_memory[None], new_factor)


def solution(mesh):
    in_specs = (P("dp", "shard", None), P("dp", "shard", None), P())
    out_specs = (P("dp", "shard", None), P())
    return jax.shard_map(
        per_device, mesh=mesh, in_specs=in_specs, out_specs=out_specs, check_vma=False
    )
```

time: 543 us -> 76.9 us (0.14)
  waiting for transfers between devices: 468 us -> 0 us
  Pallas kernels: 0 us -> 74.9 us
  matrix products: 32.7 us -> 0 us
  other arithmetic: 25.6 us -> 0 us
  between operations: 13.8 us -> 0.65 us
    psum x3 -> x0, waiting for transfers between devices: 467 us -> none  [the longest x1 261 us: per_device(): new_factor = lax.psum(local_term, ('dp', 'shard')) / replicas]
    pallas_call x0 -> x2, Pallas kernels: none -> 74.9 us  [the longest x1 67.5 us: exchange(): pl.pallas_call(exchange_kernel, out_shape=(jax.ShapeDtypeStruct((PADDED,...]
    dot_general x4 -> x0, matrix products: 31.4 us -> none  [the longest x1 13.4 us: per_device(): jnp.einsum('hd,hk->dk', corrected, orthonormal, precision=lax.Precision.H...]
    another operation x5 -> x0, other arithmetic: 22.9 us -> none  [the longest x3 12.4 us: per_device(): lower_factor = jnp.linalg.cholesky(gram_matrix)]
  transfers between devices with their start and end apart: 3 -> 0, of which waited for: 3 -> 0; matrix products, arithmetic and copies ran while one was open for 0% -> 0% of each run, Pallas kernels for 0% -> 0%
where the time goes in v1:
time: 76.9 us; the launch traced here: 76.7 us
  Pallas kernels  74.9 us (97%)
  local copies, waits for them, and re-layouts  1.21 us (2%)
    pallas_call x1, Pallas kernels, exchange(): pl.pallas_call(exchange_kernel, out_shape=(jax.ShapeDtypeStruct((PADDED,...  67.5 us
    pallas_call x1, Pallas kernels, residual(): pl.pallas_call(residual_kernel, grid=(4,), out_shape=(jax.ShapeDtypeStruc...  7.33 us

profile of v1, /device:TPU:1, one launch (start us, length us, event | category | flops | bytes accessed | tf_op | source)
XLA Modules:
  0.0 76.7 jit_solution(5348645826983951918)
XLA Ops:
  0.6 0.0 copy-start.1
  0.6 1.2 %copy-done.1 = bf16[3968,128]{1,0:T(8,128)(2,1)S(1)} copy-done((bf16[3968,128]{1,0:T(8,128)(2,1)S(1)}, bf16[3968,128]{1,0:T(8,128)(2,1)}, u32[]{:S(2)}) %copy-start.1) | copy-done | bytes 1015832
  1.8 0.0 copy-start
  1.8 67.5 %exchange.1 = (f32[4096,128]{1,0:T(8,128)S(1)}, f32[384,128]{1,0:T(8,128)S(1)}) custom-call(bf16[384,3968]{1,0:T(8,128)(2,1)} %bitcast.3, bf16[384,3968]{1,0:T(8,128)(2,1)} %bitcast.5, bf16[3968,128]{1,0:T(8,128)(2,1)S(1)} %copy-done.1), custom_call_target="tpu_custom_call" | custom-call | flops 4000000000 | bytes 10000000 | tf_op jit(solution)/shard_map/exchange/pallas_call | solution.py:290
  69.4 0.0 copy-done
  69.4 7.3 %residual.1 = (bf16[384,3968]{1,0:T(8,128)(2,1)}, f32[3968,128]{1,0:T(8,128)}) custom-call(bf16[384,3968]{1,0:T(8,128)(2,1)S(1)} %bitcast.4, bf16[384,3968]{1,0:T(8,128)(2,1)} %bitcast.6, f32[384,128]{1,0:T(8,128)S(1)} %get-tuple-element.6.o_ref, f32[4096,128]{1,0:T(8,128)S(1)} %get-tuple-element.7.n_ref), custom_call_target="tpu_custom_call" | custom-call | tf_op jit(solution)/shard_map/residual/pallas_call | solution.py:341
Async XLA Ops:
  0.6 1.2 %copy-start.1 = (bf16[3968,128]{1,0:T(8,128)(2,1)S(1)}, bf16[3968,128]{1,0:T(8,128)(2,1)}, u32[]{:S(2)}) copy-start(bf16[3968,128]{1,0:T(8,128)(2,1)} %f_hbm.1) | copy-start | bytes 3047428
  1.8 67.5 %copy-start = (bf16[1,384,3968]{2,1,0:T(8,128)(2,1)S(1)}, bf16[1,384,3968]{2,1,0:T(8,128)(2,1)}, u32[]{:S(2)}) copy-start(bf16[1,384,3968]{2,1,0:T(8,128)(2,1)} %param.3) | copy-start | bytes 9142276

commit v2 on v1

v2 whole, which is shorter than its diff:
```python
import functools

import jax
import jax.numpy as jnp
from jax import lax
from jax.experimental import pallas as pl
from jax.experimental.pallas import tpu as pltpu
from jax.sharding import PartitionSpec as P

MESH = pl.DeviceIdType.MESH
D = 3968
RANK = 128
ROWS = 384
ZS, YS, XS, CORES = 8, 4, 4, 2
DP = ZS * YS
PIECE = ROWS // DP
PADDED = 4096
HALF = PADDED // CORES
BIG = HALF // 4
MID = BIG // 4
SMALL = MID // ZS
BLOCKS = D // 128
FAR = (2, 1, 3, 0)
NEAR = (0, 1, 3, 2)
FAR_Z = (4, 3, 5, 2, 6, 1, 7, 0)
VMEM_BYTES = 48 * 1024 * 1024


def eight_columns(step, gram, inverse):
    row = lax.broadcasted_iota(jnp.int32, (RANK, 1), 0)
    row8 = lax.broadcasted_iota(jnp.int32, (8, RANK), 0)
    live = row[8:] + 8 * step < RANK
    columns = [jnp.broadcast_to(gram[:, k:k + 1], (RANK, RANK)) for k in range(8)]
    top = [column[:8] for column in columns]
    below = [jnp.where(live, column[8:], 0.0) for column in columns]
    gram8, inverse8 = gram[:8], inverse[:8]
    gram_rest, inverse_rest = gram[8:], inverse[8:]
    pivots = []
    for k in range(8):
        pivot = jnp.broadcast_to(top[k][k:k + 1], (8, RANK))
        reciprocal = 1.0 / pivot
        pivots.append(pivot[:1])
        factor8 = jnp.where(row8 > k, top[k] * reciprocal, 0.0)
        factor = below[k] * reciprocal[:1]
        for j in range(k + 1, 8):
            upper = top[j][k:k + 1]
            top[j] = top[j] - factor8 * upper
            below[j] = below[j] - factor * upper
        gram_row, inverse_row = gram8[k:k + 1], inverse8[k:k + 1]
        gram_rest = gram_rest - factor * gram_row
        inverse_rest = inverse_rest - factor * inverse_row
        gram8 = gram8 - factor8 * gram_row
        inverse8 = inverse8 - factor8 * inverse_row
    done = inverse8 * lax.rsqrt(jnp.concatenate(pivots, 0))
    inverse = jnp.concatenate([inverse_rest, done], 0)
    gram = jnp.concatenate([gram_rest, gram8], 0)
    return pltpu.roll(gram, RANK - 8, 1), inverse


def split(value):
    high = value.astype(jnp.bfloat16)
    return high, (value - high.astype(jnp.float32)).astype(jnp.bfloat16)


def land(ref, sem):
    pltpu.make_async_copy(ref, ref, sem).wait()


def exchange_kernel(g_hbm, m_hbm, f_hbm, new_ref, n_ref,
                    gm, f, gmt, part, part_in, span_all, span, span2, o2,
                    gram, gram_in, gram_x, gram_back, lower, inverse, x, core_in, a_in, z_in,
                    load_sem, part_send, part_recv, span_send, span_recv,
                    gram_send, gram_recv, core_send, core_recv, a_send, a_recv, z_send, z_recv,
                    gz_send, gz_recv, ga_send, ga_recv, gc_send, gc_recv):
    dp, shard = lax.axis_index("dp"), lax.axis_index("shard")
    zi, yi = dp // YS, dp % YS
    xi, ci = shard // CORES, shard % CORES
    a = xi * (1 - ci) + yi * ci
    b = yi * (1 - ci) + xi * ci

    def plane_peer(j):
        return (j, shard)

    def a_peer(k):
        return (zi * YS + (yi + k * ci) % 4, ((xi + k * (1 - ci)) % 4) * CORES + ci)

    def bz_peer(kb, kz):
        return (((zi + kz) % ZS) * YS + (yi + kb * (1 - ci)) % 4, ((xi + kb * ci) % 4) * CORES + ci)

    def xz_peer(kx, kz):
        return (((zi + kz) % ZS) * YS + yi, ((xi + kx) % 4) * CORES + ci)

    sibling = (dp, xi * CORES + 1 - ci)

    def send(src, dst, send_sem, recv_sem, to):
        pltpu.make_async_remote_copy(src_ref=src, dst_ref=dst, send_sem=send_sem, recv_sem=recv_sem,
                                     device_id=to, device_id_type=MESH).start()

    def greet(to):
        pl.semaphore_signal(barrier, inc=1, device_id=to, device_id_type=MESH)

    load_f = pltpu.make_async_copy(f_hbm, f, load_sem.at[8])
    load_f.start()

    def quarter(i):
        return (zi // 2 + 6 - i) % 4

    def loads(i):
        q = quarter(i)
        rows = pl.ds(pl.multiple_of(q * 96, 96), 96)
        first = pl.ds(pl.multiple_of(q * 192, 96), 96)
        second = pl.ds(pl.multiple_of(q * 192 + 96, 96), 96)
        return (pltpu.make_async_copy(g_hbm.at[rows], gm.at[first], load_sem.at[2 * i]),
                pltpu.make_async_copy(m_hbm.at[rows], gm.at[second], load_sem.at[2 * i + 1]))

    for i in range(4):
        for copy in loads(i):
            copy.start()

    barrier = pltpu.get_barrier_semaphore()

    def greet_plane(k, _):
        greet(plane_peer((dp + k) % DP))
        return 0
    lax.fori_loop(1, DP, greet_plane, 0)

    def greet_x(k, _):
        for kx in (1, 2, 3):
            greet(xz_peer(kx, k))
        return 0
    lax.fori_loop(0, 1 + (ZS - 1) * ci, greet_x, 0)
    greet(sibling)

    load_f.wait()
    for i in range(4):
        q = quarter(i)
        for copy in loads(i):
            copy.wait()
        both = jnp.dot(gm[pl.ds(pl.multiple_of(q * 192, 192), 192), :], f[...], preferred_element_type=jnp.float32)
        value = both[:96] + both[96:]
        for j in range(8):
            part[q * 8 + j] = value[PIECE * j:PIECE * (j + 1)]
        if i == 0:
            pl.semaphore_wait(barrier, DP + 3 + 3 * (ZS - 1) * ci)

        def scatter(j, _):
            to = q * 8 + j

            @pl.when(to != dp)
            def _():
                send(part.at[to], part_in.at[(to - dp + DP) % DP - 1], part_send, part_recv, plane_peer(to))
            return 0
        lax.fori_loop(0, 8, scatter, 0)

    def turn(i, _):
        lanes = pl.ds(pl.multiple_of(i * 128, 128), 128)
        gmt[lanes, :] = gm[:, lanes].T
        return 0
    lax.fori_loop(0, BLOCKS, turn, 0)
    gmt[D:, :] = jnp.zeros((PADDED - D, 2 * ROWS), jnp.bfloat16)

    land(part_in, part_recv)
    total = part[dp]
    for k in range(DP - 1):
        total = total + part_in[k]
    span_all[dp] = total * (1.0 / DP)

    def spread(k, _):
        send(span_all.at[dp], span_all.at[dp], span_send, span_recv, plane_peer((dp + k) % DP))
        return 0
    lax.fori_loop(1, DP, spread, 0)
    land(span_all.at[pl.ds(0, DP - 1)], span_recv)

    for j in range(DP // 2):
        span[24 * j:24 * (j + 1), :] = jnp.concatenate([span_all[2 * j], span_all[2 * j + 1]], 0)
    for q in range(4):
        high, low = split(span[96 * q:96 * (q + 1), :])
        for start in (192 * q, 192 * q + 96):
            span2[start:start + 96, :RANK] = high
            span2[start:start + 96, RANK:] = low

    mine = pl.ds(pl.multiple_of(ci * 64, 64), 64)
    other = pl.ds(pl.multiple_of((1 - ci) * 64, 64), 64)

    def product(start):
        both = jnp.dot(gmt[pl.ds(start, BIG), :], span2[...], preferred_element_type=jnp.float32)
        return both[:, :RANK] + both[:, RANK:]

    def for_sibling(i):
        start = pl.multiple_of((1 - ci) * HALF + ((b + FAR[i]) % 4) * BIG, BIG)
        x[pl.ds(start, BIG), :] = product(start)
        send(x.at[pl.ds(start, BIG)], core_in.at[i], core_send, core_recv.at[i], sibling)

    def for_axis(i):
        start = pl.multiple_of(ci * HALF + ((a + FAR[i]) % 4) * BIG, BIG)
        value = product(start)
        land(core_in.at[i], core_recv.at[i])
        x[pl.ds(start, BIG), :] = value + core_in[i]
        if FAR[i]:
            for j, kb in enumerate(FAR):
                rows = pl.ds(pl.multiple_of(start + ((b + kb) % 4) * MID, MID), MID)
                send(x.at[rows], a_in.at[i, j], a_send, a_recv.at[i, j], a_peer(FAR[i]))

    for_sibling(0)
    gram[...] = lax.dot_general(span[...], span[...], (((0,), (0,)), ((), ())),
                                precision=lax.Precision.HIGHEST, preferred_element_type=jnp.float32)
    send(gram.at[other], gram_in, gram_send.at[0], gram_recv.at[0], sibling)
    for_sibling(1)
    for_axis(0)
    land(gram_in, gram_recv.at[0])
    gram[mine, :] = gram[mine, :] + gram_in[...]
    for r in (1, 2, 3):
        send(gram.at[mine], gram_x.at[r - 1], gram_send.at[1], gram_recv.at[1], xz_peer(r, 0))
    for_sibling(2)
    for_axis(1)
    for_sibling(3)
    for_axis(2)
    for_axis(3)

    land(gram_x, gram_recv.at[1])
    land(gram_x, gram_send.at[1])
    gram[mine, :] = gram[mine, :] + gram_x[0] + gram_x[1] + gram_x[2]
    send(gram.at[mine], gram_back, gram_send.at[2], gram_recv.at[2], sibling)
    lower[mine, :] = gram[mine, :]
    row = lax.broadcasted_iota(jnp.int32, (RANK, RANK), 0)
    lane = lax.broadcasted_iota(jnp.int32, (RANK, RANK), 1)
    inverse[...] = (row == lane).astype(jnp.float32)

    def eliminate(first, last):
        def one(step, _):
            lower[...], inverse[...] = eight_columns(step, lower[...], inverse[...])
            return 0
        lax.fori_loop(first, last, one, 0)

    own = pl.multiple_of(ci * HALF + a * BIG, BIG)
    for j, kb in enumerate(FAR):
        block = pl.multiple_of(own + ((b + kb) % 4) * MID, MID)
        rows = pl.ds(block, MID)
        for i in range(3):
            land(a_in.at[i, j], a_recv.at[i, j])
        x[rows, :] = x[rows, :] + a_in[0, j] + a_in[1, j] + a_in[2, j]
        for kz in FAR_Z:
            if kb or kz:
                piece = pl.ds(pl.multiple_of(block + ((zi + kz) % ZS) * SMALL, SMALL), SMALL)
                slot = ZS * j + kz - (1 if kb == 0 else 0)
                send(x.at[piece], z_in.at[slot], z_send, z_recv, bz_peer(kb, kz))
        if j == 0:
            land(gram_back, gram_recv.at[2])
            lower[other, :] = gram_back[...]
        eliminate(2 * j, 2 * j + 2)
    eliminate(8, 16)
    span_in_basis = lax.dot_general(span[...], inverse[...], (((1,), (1,)), ((), ())),
                                    precision=lax.Precision.HIGHEST, preferred_element_type=jnp.float32)
    high, low = split(span_in_basis)
    o2[:, :RANK] = high
    o2[:, RANK:] = low
    last = pl.ds(pl.multiple_of(own + b * MID + zi * SMALL, SMALL), SMALL)
    land(z_in, z_recv)
    total = x[last, :]
    for k in range(4 * ZS - 1):
        total = total + z_in[k]

    n_ref[last, :] = lax.dot_general(total * (1.0 / DP), inverse[...], (((1,), (1,)), ((), ())),
                                     precision=lax.Precision.HIGHEST, preferred_element_type=jnp.float32)
    for j, kb in enumerate(NEAR):
        for kz in FAR_Z:
            if kb or kz:
                send(n_ref.at[last], n_ref.at[last], gz_send, gz_recv.at[j], bz_peer(kb, kz))

    def block_of(core, first, second):
        return pl.multiple_of(core * HALF + first * BIG + second * MID, MID)

    def residual(start):
        @pl.when(start < D)
        def _():
            cols = pl.ds(start, MID)
            high, low = split(n_ref[cols, :])
            update = (lax.dot_general(o2[...], jnp.concatenate([high, high], 1), (((1,), (1,)), ((), ())),
                                      preferred_element_type=jnp.float32)
                      + lax.dot_general(o2[:, :RANK], low, (((1,), (1,)), ((), ())),
                                        preferred_element_type=jnp.float32))
            for q in range(4):
                corrected = (gm[192 * q:192 * q + 96, cols].astype(jnp.float32)
                             + gm[192 * q + 96:192 * q + 192, cols].astype(jnp.float32))
                new_ref[96 * q:96 * (q + 1), cols] = (corrected - update[96 * q:96 * (q + 1)]).astype(jnp.bfloat16)

    arrivals = [(i, j) for i in (3,) for j in range(4)] + [(i, j) for j in range(4) for i in range(3)]

    def take_own(i, j):
        if i == 3:
            start = block_of(ci, a, (b - NEAR[j] + 4) % 4)
            here = pl.ds(start, MID)
            land(n_ref.at[pl.ds(0, (ZS - 1) * SMALL if NEAR[j] == 0 else MID)], gz_recv.at[j])
            for r in range(3):
                send(n_ref.at[here], n_ref.at[here], ga_send, ga_recv.at[r, j], a_peer(FAR[r]))
        else:
            start = block_of(ci, (a - FAR[i] + 4) % 4, (b - NEAR[j] + 4) % 4)
            here = pl.ds(start, MID)
            land(n_ref.at[here], ga_recv.at[i, j])
        send(n_ref.at[here], n_ref.at[here], gc_send, gc_recv.at[i, j], sibling)
        return start

    def take_sibling(i, j):
        start = block_of(1 - ci, (b - FAR[i] + 4) % 4, (a - NEAR[j] + 4) % 4)
        land(n_ref.at[pl.ds(start, MID)], gc_recv.at[i, j])
        residual(start)

    for n, (i, j) in enumerate(arrivals):
        start = take_own(i, j)
        residual(start)
        if n >= 4:
            take_sibling(*arrivals[n - 4])
    for i, j in arrivals[-4:]:
        take_sibling(i, j)

    land(part_in, part_send)
    land(part_in, span_send)
    land(gram_in, gram_send.at[0])
    land(gram_in, gram_send.at[2])
    land(x.at[pl.ds(0, HALF)], core_send)
    land(a_in, a_send)
    land(z_in, z_send)
    land(z_in, gz_send)
    land(a_in, ga_send)
    land(x.at[pl.ds(0, HALF)], gc_send)


def exchange(g, m, f):
    dma = pltpu.SemaphoreType.DMA
    f32, bf16 = jnp.float32, jnp.bfloat16
    return pl.pallas_call(
        exchange_kernel,
        out_shape=(jax.ShapeDtypeStruct((ROWS, D), bf16), jax.ShapeDtypeStruct((PADDED, RANK), f32)),
        in_specs=[pl.BlockSpec(memory_space=pltpu.HBM)] * 3,
        out_specs=(pl.BlockSpec(memory_space=pltpu.VMEM), pl.BlockSpec(memory_space=pltpu.VMEM)),
        scratch_shapes=[
            pltpu.VMEM((2 * ROWS, D), bf16), pltpu.VMEM((D, RANK), bf16), pltpu.VMEM((PADDED, 2 * ROWS), bf16),
            pltpu.VMEM((DP, PIECE, RANK), f32), pltpu.VMEM((DP - 1, PIECE, RANK), f32),
            pltpu.VMEM((DP, PIECE, RANK), f32), pltpu.VMEM((ROWS, RANK), f32),
            pltpu.VMEM((2 * ROWS, 2 * RANK), bf16), pltpu.VMEM((ROWS, 2 * RANK), bf16),
            pltpu.VMEM((RANK, RANK), f32), pltpu.VMEM((64, RANK), f32), pltpu.VMEM((3, 64, RANK), f32),
            pltpu.VMEM((64, RANK), f32), pltpu.VMEM((RANK, RANK), f32), pltpu.VMEM((RANK, RANK), f32),
            pltpu.VMEM((PADDED, RANK), f32), pltpu.VMEM((4, BIG, RANK), f32),
            pltpu.VMEM((3, 4, MID, RANK), f32), pltpu.VMEM((4 * ZS - 1, SMALL, RANK), f32),
            dma((9,)), dma, dma, dma, dma, dma((3,)), dma((3,)), dma, dma((4,)), dma, dma((3, 4)), dma, dma,
            dma, dma((4,)), dma, dma((3, 4)), dma, dma((4, 4)),
        ],
        compiler_params=pltpu.CompilerParams(collective_id=0, has_side_effects=True, vmem_limit_bytes=VMEM_BYTES),
        cost_estimate=pl.CostEstimate(flops=4 * 10 ** 9, bytes_accessed=10 ** 7, transcendentals=0),
        name="exchange",
    )(g, m, f)


def per_device(gradient, memory, old_factor):
    new_memory, new_factor = exchange(gradient[0], memory[0], old_factor)
    return (new_memory[None], new_factor[:D])


def solution(mesh):
    in_specs = (P("dp", "shard", None), P("dp", "shard", None), P())
    out_specs = (P("dp", "shard", None), P())
    return jax.shard_map(
        per_device, mesh=mesh, in_specs=in_specs, out_specs=out_specs, check_vma=False
    )
```

time: 76.9 us -> 69.8 us (0.908)
  Pallas kernels: 74.9 us -> 64.8 us
  local copies, waits for them, and re-layouts: 1.21 us -> 4.26 us
    pallas_call x2 -> x1, Pallas kernels: 74.9 us -> 64.8 us  [exchange(): pl.pallas_call(exchange_kernel, out_shape=(jax.ShapeDtypeStruct((ROWS, D)...]
    unnamed x4 -> x3, local copies, waits for them, and re-layouts: 1.21 us -> 2.84 us
    slice x0 -> x1, local copies, waits for them, and re-layouts: none -> 1.42 us  [per_device(): return (new_memory[None], new_factor[:D])]
where the time goes in v2:
time: 69.8 us; the launch traced here: 69.7 us
  Pallas kernels  64.8 us (93%)
  local copies, waits for them, and re-layouts  4.26 us (6%)
    pallas_call x1, Pallas kernels, exchange(): pl.pallas_call(exchange_kernel, out_shape=(jax.ShapeDtypeStruct((ROWS, D)...  64.8 us
    unnamed x3, local copies, waits for them, and re-layouts  2.84 us
    slice x1, local copies, waits for them, and re-layouts, per_device(): return (new_memory[None], new_factor[:D])  1.42 us

profile of v2, /device:TPU:1, one launch (start us, length us, event | category | flops | bytes accessed | tf_op | source)
XLA Modules:
  0.0 69.7 jit_solution(4326732662023202281)
XLA Ops:
  0.6 0.0 copy-start
  0.6 1.2 %copy-done = bf16[3968,128]{1,0:T(8,128)(2,1)S(1)} copy-done((bf16[3968,128]{1,0:T(8,128)(2,1)S(1)}, bf16[3968,128]{1,0:T(8,128)(2,1)}, u32[]{:S(2)}) %copy-start) | copy-done | bytes 1015832
  1.8 64.8 %exchange.1 = (bf16[384,3968]{1,0:T(8,128)(2,1)S(1)}, f32[4096,128]{1,0:T(8,128)S(1)}) custom-call(bf16[384,3968]{1,0:T(8,128)(2,1)} %bitcast.4, bf16[384,3968]{1,0:T(8,128)(2,1)} %bitcast.5, bf16[3968,128]{1,0:T(8,128)(2,1)S(1)} %copy-done), custom_call_target="tpu_custom_call" | custom-call | flops 4000000000 | bytes 10000000 | tf_op jit(solution)/shard_map/exchange/pallas_call | solution.py:331
  66.7 1.4 %slice.3 = f32[3968,128]{1,0:T(8,128)} slice(f32[4096,128]{1,0:T(8,128)S(1)} %get-tuple-element.5), slice={[0:3968], [0:128]} | slice | bytes 4063232 | tf_op jit(solution)/shard_map/slice | solution.py:356
  68.1 1.6 %copy.6 = bf16[1,384,3968]{2,1,0:T(8,128)(2,1)} copy(bf16[1,384,3968]{2,1,0:T(8,128)(2,1)S(1)} %bitcast.3) | data formatting | bytes 6094848
Async XLA Ops:
  0.6 1.2 %copy-start = (bf16[3968,128]{1,0:T(8,128)(2,1)S(1)}, bf16[3968,128]{1,0:T(8,128)(2,1)}, u32[]{:S(2)}) copy-start(bf16[3968,128]{1,0:T(8,128)(2,1)} %f_hbm.1) | copy-start | bytes 3047428

commit v3 on v2

--- a/solution.py
+++ b/solution.py
@@ -24,13 +24,15 @@
 NEAR = (0, 1, 3, 2)
 FAR_Z = (4, 3, 5, 2, 6, 1, 7, 0)
 VMEM_BYTES = 48 * 1024 * 1024
-
-
-def eight_columns(step, gram, inverse):
-    row = lax.broadcasted_iota(jnp.int32, (RANK, 1), 0)
+STORE_VMEM = 16 * 1024 * 1024
+
+
+def eight_columns(live_from, gram, inverse):
+    size = gram.shape[0]
+    row = lax.broadcasted_iota(jnp.int32, (size, 1), 0)
     row8 = lax.broadcasted_iota(jnp.int32, (8, RANK), 0)
-    live = row[8:] + 8 * step < RANK
-    columns = [jnp.broadcast_to(gram[:, k:k + 1], (RANK, RANK)) for k in range(8)]
+    live = row[8:] < live_from
+    columns = [jnp.broadcast_to(gram[:, k:k + 1], (size, RANK)) for k in range(8)]
     top = [column[:8] for column in columns]
     below = [jnp.where(live, column[8:], 0.0) for column in columns]
     gram8, inverse8 = gram[:8], inverse[:8]
@@ -52,9 +54,8 @@
         gram8 = gram8 - factor8 * gram_row
         inverse8 = inverse8 - factor8 * inverse_row
     done = inverse8 * lax.rsqrt(jnp.concatenate(pivots, 0))
-    inverse = jnp.concatenate([inverse_rest, done], 0)
-    gram = jnp.concatenate([gram_rest, gram8], 0)
-    return pltpu.roll(gram, RANK - 8, 1), inverse
+    gram = pltpu.roll(jnp.concatenate([gram_rest, gram8], 0), RANK - 8, 1)
+    return gram, jnp.concatenate([inverse_rest, inverse8], 0), done
 
 
 def split(value):
@@ -66,10 +67,10 @@
     pltpu.make_async_copy(ref, ref, sem).wait()
 
 
-def exchange_kernel(g_hbm, m_hbm, f_hbm, new_ref, n_ref,
-                    gm, f, gmt, part, part_in, span_all, span, span2, o2,
-                    gram, gram_in, gram_x, gram_back, lower, inverse, x, core_in, a_in, z_in,
-                    load_sem, part_send, part_recv, span_send, span_recv,
+def exchange_kernel(g_hbm, m_hbm, f, new_ref, n_ref,
+                    gm, gmt, part, part_y, part_z, span_all, span, span2, o2,
+                    gram, gram_in, gram_x, gram_back, lower, work, inverse, x, core_in, a_in, z_in,
+                    load_sem, party_send, party_recv, part_send, part_recv, span_send, span_recv,
                     gram_send, gram_recv, core_send, core_recv, a_send, a_recv, z_send, z_recv,
                     gz_send, gz_recv, ga_send, ga_recv, gc_send, gc_recv):
     dp, shard = lax.axis_index("dp"), lax.axis_index("shard")
@@ -84,6 +85,9 @@
     def a_peer(k):
         return (zi * YS + (yi + k * ci) % 4, ((xi + k * (1 - ci)) % 4) * CORES + ci)
 
+    def y_peer(k):
+        return (zi * YS + (yi + k) % YS, shard)
+
     def bz_peer(kb, kz):
         return (((zi + kz) % ZS) * YS + (yi + kb * (1 - ci)) % 4, ((xi + kb * ci) % 4) * CORES + ci)
 
@@ -99,11 +103,9 @@
     def greet(to):
         pl.semaphore_signal(barrier, inc=1, device_id=to, device_id_type=MESH)
 
-    load_f = pltpu.make_async_copy(f_hbm, f, load_sem.at[8])
-    load_f.start()
 
     def quarter(i):
-        return (zi // 2 + 6 - i) % 4
+        return (yi + FAR[i]) % 4
 
     def loads(i):
         q = quarter(i)
@@ -118,57 +120,55 @@
             copy.start()
 
     barrier = pltpu.get_barrier_semaphore()
-
-    def greet_plane(k, _):
-        greet(plane_peer((dp + k) % DP))
-        return 0
-    lax.fori_loop(1, DP, greet_plane, 0)
-
-    def greet_x(k, _):
-        for kx in (1, 2, 3):
-            greet(xz_peer(kx, k))
-        return 0
-    lax.fori_loop(0, 1 + (ZS - 1) * ci, greet_x, 0)
+    for k in (4, 3, 5, 2, 6, 1, 7):
+        greet(xz_peer(0, k))
+    for k in (2, 1, 3):
+        greet(y_peer(k))
+        greet(xz_peer(k, 0))
     greet(sibling)
 
-    load_f.wait()
     for i in range(4):
         q = quarter(i)
         for copy in loads(i):
             copy.wait()
-        both = jnp.dot(gm[pl.ds(pl.multiple_of(q * 192, 192), 192), :], f[...], preferred_element_type=jnp.float32)
+        both = jnp.dot(gm[pl.ds(pl.multiple_of(q * 192, 192), 192), :], f[:D, :], preferred_element_type=jnp.float32)
         value = both[:96] + both[96:]
-        for j in range(8):
-            part[q * 8 + j] = value[PIECE * j:PIECE * (j + 1)]
+        for j in range(ZS):
+            part[q * ZS + j] = value[PIECE * j:PIECE * (j + 1)]
         if i == 0:
-            pl.semaphore_wait(barrier, DP + 3 + 3 * (ZS - 1) * ci)
-
-        def scatter(j, _):
-            to = q * 8 + j
-
-            @pl.when(to != dp)
-            def _():
-                send(part.at[to], part_in.at[(to - dp + DP) % DP - 1], part_send, part_recv, plane_peer(to))
-            return 0
-        lax.fori_loop(0, 8, scatter, 0)
+            pl.semaphore_wait(barrier, 14)
+        if FAR[i]:
+            send(part.at[pl.ds(q * ZS, ZS)], part_y.at[i], party_send, party_recv.at[i], y_peer(FAR[i]))
 
     def turn(i, _):
         lanes = pl.ds(pl.multiple_of(i * 128, 128), 128)
         gmt[lanes, :] = gm[:, lanes].T
         return 0
-    lax.fori_loop(0, BLOCKS, turn, 0)
+    lax.fori_loop(0, BLOCKS // 2, turn, 0)
+    for i in range(3):
+        land(part_y.at[i], party_recv.at[i])
+    for j in range(ZS):
+        to = (zi + FAR_Z[j]) % ZS
+        slot = yi * ZS + to
+        part[slot] = (part[slot] + part_y[0, to]) + (part_y[1, to] + part_y[2, to])
+        if FAR_Z[j]:
+            send(part.at[slot], part_z.at[FAR_Z[j] - 1], part_send, part_recv, xz_peer(0, FAR_Z[j]))
+    lax.fori_loop(BLOCKS // 2, BLOCKS, turn, 0)
     gmt[D:, :] = jnp.zeros((PADDED - D, 2 * ROWS), jnp.bfloat16)
 
-    land(part_in, part_recv)
-    total = part[dp]
-    for k in range(DP - 1):
-        total = total + part_in[k]
-    span_all[dp] = total * (1.0 / DP)
+    me = yi * ZS + zi
+    land(part_z, part_recv)
+    total = part[me]
+    for k in range(ZS - 1):
+        total = total + part_z[k]
+    span_all[me] = total * (1.0 / DP)
 
     def spread(k, _):
-        send(span_all.at[dp], span_all.at[dp], span_send, span_recv, plane_peer((dp + k) % DP))
+        send(span_all.at[me], span_all.at[me], span_send, span_recv, plane_peer((dp + k) % DP))
         return 0
-    lax.fori_loop(1, DP, spread, 0)
+    lax.fori_loop(10, 23, spread, 0)
+    lax.fori_loop(1, 10, spread, 0)
+    lax.fori_loop(23, DP, spread, 0)
     land(span_all.at[pl.ds(0, DP - 1)], span_recv)
 
     for j in range(DP // 2):
@@ -201,34 +201,32 @@
                 rows = pl.ds(pl.multiple_of(start + ((b + kb) % 4) * MID, MID), MID)
                 send(x.at[rows], a_in.at[i, j], a_send, a_recv.at[i, j], a_peer(FAR[i]))
 
-    for_sibling(0)
     gram[...] = lax.dot_general(span[...], span[...], (((0,), (0,)), ((), ())),
                                 precision=lax.Precision.HIGHEST, preferred_element_type=jnp.float32)
     send(gram.at[other], gram_in, gram_send.at[0], gram_recv.at[0], sibling)
+    for_sibling(0)
     for_sibling(1)
-    for_axis(0)
     land(gram_in, gram_recv.at[0])
     gram[mine, :] = gram[mine, :] + gram_in[...]
     for r in (1, 2, 3):
         send(gram.at[mine], gram_x.at[r - 1], gram_send.at[1], gram_recv.at[1], xz_peer(r, 0))
+    for_axis(0)
     for_sibling(2)
     for_axis(1)
     for_sibling(3)
     for_axis(2)
     for_axis(3)
-
-    land(gram_x, gram_recv.at[1])
-    land(gram_x, gram_send.at[1])
-    gram[mine, :] = gram[mine, :] + gram_x[0] + gram_x[1] + gram_x[2]
-    send(gram.at[mine], gram_back, gram_send.at[2], gram_recv.at[2], sibling)
-    lower[mine, :] = gram[mine, :]
     row = lax.broadcasted_iota(jnp.int32, (RANK, RANK), 0)
     lane = lax.broadcasted_iota(jnp.int32, (RANK, RANK), 1)
-    inverse[...] = (row == lane).astype(jnp.float32)
+    work[...] = (row == lane).astype(jnp.float32)
 
     def eliminate(first, last):
+        size = RANK - 32 * (first // 4)
+
         def one(step, _):
-            lower[...], inverse[...] = eight_columns(step, lower[...], inverse[...])
+            rows = pl.ds(pl.multiple_of(step * 8, 8), 8)
+            lower[:size, :], work[:size, :], inverse[rows, :] = eight_columns(
+                RANK - 8 * step, lower[:size, :], work[:size, :])
             return 0
         lax.fori_loop(first, last, one, 0)
 
@@ -245,10 +243,21 @@
                 slot = ZS * j + kz - (1 if kb == 0 else 0)
                 send(x.at[piece], z_in.at[slot], z_send, z_recv, bz_peer(kb, kz))
         if j == 0:
+            land(gram_x, gram_recv.at[1])
+            land(gram_x, gram_send.at[1])
+            gram[mine, :] = gram[mine, :] + gram_x[0] + gram_x[1] + gram_x[2]
+            send(gram.at[mine], gram_back, gram_send.at[2], gram_recv.at[2], sibling)
+            lower[mine, :] = gram[mine, :]
+        if j == 1:
             land(gram_back, gram_recv.at[2])
             lower[other, :] = gram_back[...]
-        eliminate(2 * j, 2 * j + 2)
-    eliminate(8, 16)
+            eliminate(0, 1)
+        if j == 2:
+            eliminate(1, 3)
+    eliminate(3, 4)
+    eliminate(4, 8)
+    eliminate(8, 12)
+    eliminate(12, 16)
     span_in_basis = lax.dot_general(span[...], inverse[...], (((1,), (1,)), ((), ())),
                                     precision=lax.Precision.HIGHEST, preferred_element_type=jnp.float32)
     high, low = split(span_in_basis)
@@ -313,8 +322,9 @@
     for i, j in arrivals[-4:]:
         take_sibling(i, j)
 
-    land(part_in, part_send)
-    land(part_in, span_send)
+    land(part_y, party_send)
+    land(part_z, part_send)
+    land(span_all.at[pl.ds(0, DP - 1)], span_send)
     land(gram_in, gram_send.at[0])
     land(gram_in, gram_send.at[2])
     land(x.at[pl.ds(0, HALF)], core_send)
@@ -331,18 +341,20 @@
     return pl.pallas_call(
         exchange_kernel,
         out_shape=(jax.ShapeDtypeStruct((ROWS, D), bf16), jax.ShapeDtypeStruct((PADDED, RANK), f32)),
-        in_specs=[pl.BlockSpec(memory_space=pltpu.HBM)] * 3,
+        in_specs=[pl.BlockSpec(memory_space=pltpu.HBM)] * 2 + [pl.BlockSpec(memory_space=pltpu.VMEM)],
         out_specs=(pl.BlockSpec(memory_space=pltpu.VMEM), pl.BlockSpec(memory_space=pltpu.VMEM)),
         scratch_shapes=[
-            pltpu.VMEM((2 * ROWS, D), bf16), pltpu.VMEM((D, RANK), bf16), pltpu.VMEM((PADDED, 2 * ROWS), bf16),
-            pltpu.VMEM((DP, PIECE, RANK), f32), pltpu.VMEM((DP - 1, PIECE, RANK), f32),
+            pltpu.VMEM((2 * ROWS, D), bf16), pltpu.VMEM((PADDED, 2 * ROWS), bf16),
+            pltpu.VMEM((DP, PIECE, RANK), f32), pltpu.VMEM((3, ZS, PIECE, RANK), f32),
+            pltpu.VMEM((ZS - 1, PIECE, RANK), f32),
             pltpu.VMEM((DP, PIECE, RANK), f32), pltpu.VMEM((ROWS, RANK), f32),
             pltpu.VMEM((2 * ROWS, 2 * RANK), bf16), pltpu.VMEM((ROWS, 2 * RANK), bf16),
             pltpu.VMEM((RANK, RANK), f32), pltpu.VMEM((64, RANK), f32), pltpu.VMEM((3, 64, RANK), f32),
             pltpu.VMEM((64, RANK), f32), pltpu.VMEM((RANK, RANK), f32), pltpu.VMEM((RANK, RANK), f32),
+            pltpu.VMEM((RANK, RANK), f32),
             pltpu.VMEM((PADDED, RANK), f32), pltpu.VMEM((4, BIG, RANK), f32),
             pltpu.VMEM((3, 4, MID, RANK), f32), pltpu.VMEM((4 * ZS - 1, SMALL, RANK), f32),
-            dma((9,)), dma, dma, dma, dma, dma((3,)), dma((3,)), dma, dma((4,)), dma, dma((3, 4)), dma, dma,
+            dma((8,)), dma, dma((3,)), dma, dma, dma, dma, dma((3,)), dma((3,)), dma, dma((4,)), dma, dma((3, 4)), dma, dma,
             dma, dma((4,)), dma, dma((3, 4)), dma, dma((4, 4)),
         ],
         compiler_params=pltpu.CompilerParams(collective_id=0, has_side_effects=True, vmem_limit_bytes=VMEM_BYTES),
@@ -351,9 +363,33 @@
     )(g, m, f)
 
 
+def store_kernel(new_ref, n_ref, memory_ref, factor_ref, sems):
+    copies = [pltpu.make_async_copy(new_ref.at[pl.ds(96 * i, 96)], memory_ref.at[pl.ds(96 * i, 96)], sems.at[i])
+              for i in range(4)]
+    quarter = D // 4
+    copies += [pltpu.make_async_copy(n_ref.at[pl.ds(quarter * i, quarter)], factor_ref.at[pl.ds(quarter * i, quarter)],
+                                     sems.at[4 + i]) for i in range(4)]
+    for copy in copies:
+        copy.start()
+    for copy in copies:
+        copy.wait()
+
+
+def store(new, n):
+    return pl.pallas_call(
+        store_kernel,
+        out_shape=(jax.ShapeDtypeStruct((ROWS, D), jnp.bfloat16), jax.ShapeDtypeStruct((D, RANK), jnp.float32)),
+        in_specs=[pl.BlockSpec(memory_space=pltpu.VMEM)] * 2,
+        out_specs=(pl.BlockSpec(memory_space=pltpu.HBM), pl.BlockSpec(memory_space=pltpu.HBM)),
+        scratch_shapes=[pltpu.SemaphoreType.DMA((8,))],
+        compiler_params=pltpu.CompilerParams(vmem_limit_bytes=STORE_VMEM),
+        name="store",
+    )(new, n)
+
+
 def per_device(gradient, memory, old_factor):
-    new_memory, new_factor = exchange(gradient[0], memory[0], old_factor)
-    return (new_memory[None], new_factor[:D])
+    new_memory, new_factor = store(*exchange(gradient[0], memory[0], old_factor))
+    return (new_memory[None], new_factor)
 
 
 def solution(mesh):

time: 69.8 us -> 65.9 us (0.944)
  local copies, waits for them, and re-layouts: 4.26 us -> 1.21 us
  Pallas kernels: 64.8 us -> 63.9 us
    pallas_call x1, Pallas kernels: 64.8 us -> 61.6 us  [exchange(): pl.pallas_call(exchange_kernel, out_shape=(jax.ShapeDtypeStruct((ROWS, D)...]
    pallas_call x0 -> x1, Pallas kernels: none -> 2.36 us  [store(): pl.pallas_call(store_kernel, out_shape=(jax.ShapeDtypeStruct((ROWS, D), j...]
    unnamed x3 -> x2, local copies, waits for them, and re-layouts: 2.84 us -> 1.21 us
    slice x1 -> x0, local copies, waits for them, and re-layouts: 1.42 us -> none  [per_device(): return (new_memory[None], new_factor[:D])]
where the time goes in v3:
time: 65.9 us; the launch traced here: 65.8 us
  Pallas kernels  63.9 us (97%)
  local copies, waits for them, and re-layouts  1.21 us (2%)
    pallas_call x1, Pallas kernels, exchange(): pl.pallas_call(exchange_kernel, out_shape=(jax.ShapeDtypeStruct((ROWS, D)...  61.6 us
    pallas_call x1, Pallas kernels, store(): pl.pallas_call(store_kernel, out_shape=(jax.ShapeDtypeStruct((ROWS, D), j...  2.36 us

profile of v3, /device:TPU:1, one launch (start us, length us, event | category | flops | bytes accessed | tf_op | source)
XLA Modules:
  0.0 65.8 jit_solution(8627078663629398971)
XLA Ops:
  0.6 0.0 copy-start
  0.6 1.2 %copy-done = bf16[3968,128]{1,0:T(8,128)(2,1)S(1)} copy-done((bf16[3968,128]{1,0:T(8,128)(2,1)S(1)}, bf16[3968,128]{1,0:T(8,128)(2,1)}, u32[]{:S(2)}) %copy-start) | copy-done | bytes 1015832
  1.8 61.6 %exchange.1 = (bf16[384,3968]{1,0:T(8,128)(2,1)S(1)}, f32[4096,128]{1,0:T(8,128)S(1)}) custom-call(bf16[384,3968]{1,0:T(8,128)(2,1)} %bitcast.3, bf16[384,3968]{1,0:T(8,128)(2,1)} %bitcast.4, bf16[3968,128]{1,0:T(8,128)(2,1)S(1)} %copy-done), custom_call_target="tpu_custom_call" | custom-call | flops 4000000000 | bytes 10000000 | tf_op jit(solution)/shard_map/exchange/pallas_call | solution.py:341
  63.4 2.4 %store.1 = (bf16[384,3968]{1,0:T(8,128)(2,1)}, f32[3968,128]{1,0:T(8,128)}) custom-call(bf16[384,3968]{1,0:T(8,128)(2,1)S(1)} %get-tuple-element.6.new_ref, f32[4096,128]{1,0:T(8,128)S(1)} %get-tuple-element.7.n_ref), custom_call_target="tpu_custom_call" | custom-call | tf_op jit(solution)/shard_map/store/pallas_call | solution.py:379
Async XLA Ops:
  0.6 1.2 %copy-start = (bf16[3968,128]{1,0:T(8,128)(2,1)S(1)}, bf16[3968,128]{1,0:T(8,128)(2,1)}, u32[]{:S(2)}) copy-start(bf16[3968,128]{1,0:T(8,128)(2,1)} %f.1) | copy-start | bytes 3047428

commit v4 on v3

--- a/solution.py
+++ b/solution.py
@@ -17,11 +17,12 @@
 PADDED = 4096
 HALF = PADDED // CORES
 BIG = HALF // 4
-MID = BIG // 4
-SMALL = MID // ZS
+HALF_BIG = BIG // 2
+PAIR = HALF_BIG // 2
+GROUP = PAIR // 2
+SMALL = GROUP // ZS
 BLOCKS = D // 128
 FAR = (2, 1, 3, 0)
-NEAR = (0, 1, 3, 2)
 FAR_Z = (4, 3, 5, 2, 6, 1, 7, 0)
 VMEM_BYTES = 48 * 1024 * 1024
 STORE_VMEM = 16 * 1024 * 1024
@@ -67,8 +68,8 @@
     pltpu.make_async_copy(ref, ref, sem).wait()
 
 
-def exchange_kernel(g_hbm, m_hbm, f, new_ref, n_ref,
-                    gm, gmt, part, part_y, part_z, span_all, span, span2, o2,
+def exchange_kernel(g_hbm, m_hbm, f_hbm, new_ref, n_ref,
+                    gm, f, gmt, part, part_y, part_z, span_all, span, span2, o2,
                     gram, gram_in, gram_x, gram_back, lower, work, inverse, x, core_in, a_in, z_in,
                     load_sem, party_send, party_recv, part_send, part_recv, span_send, span_recv,
                     gram_send, gram_recv, core_send, core_recv, a_send, a_recv, z_send, z_recv,
@@ -88,8 +89,9 @@
     def y_peer(k):
         return (zi * YS + (yi + k) % YS, shard)
 
-    def bz_peer(kb, kz):
-        return (((zi + kz) % ZS) * YS + (yi + kb * (1 - ci)) % 4, ((xi + kb * ci) % 4) * CORES + ci)
+    def bz_peer(flip, kz):
+        at = flipped(b, flip)
+        return (((zi + kz) % ZS) * YS + yi * ci + at * (1 - ci), (xi * (1 - ci) + at * ci) * CORES + ci)
 
     def xz_peer(kx, kz):
         return (((zi + kz) % ZS) * YS + yi, ((xi + kx) % 4) * CORES + ci)
@@ -115,7 +117,9 @@
         return (pltpu.make_async_copy(g_hbm.at[rows], gm.at[first], load_sem.at[2 * i]),
                 pltpu.make_async_copy(m_hbm.at[rows], gm.at[second], load_sem.at[2 * i + 1]))
 
-    for i in range(4):
+    load_f = pltpu.make_async_copy(f_hbm, f, load_sem.at[8])
+    load_f.start()
+    for i in range(2):
         for copy in loads(i):
             copy.start()
 
@@ -127,11 +131,15 @@
         greet(xz_peer(k, 0))
     greet(sibling)
 
+    load_f.wait()
     for i in range(4):
         q = quarter(i)
         for copy in loads(i):
             copy.wait()
-        both = jnp.dot(gm[pl.ds(pl.multiple_of(q * 192, 192), 192), :], f[:D, :], preferred_element_type=jnp.float32)
+        if i < 2:
+            for copy in loads(i + 2):
+                copy.start()
+        both = jnp.dot(gm[pl.ds(pl.multiple_of(q * 192, 192), 192), :], f[...], preferred_element_type=jnp.float32)
         value = both[:96] + both[96:]
         for j in range(ZS):
             part[q * ZS + j] = value[PIECE * j:PIECE * (j + 1)]
@@ -191,15 +199,27 @@
         x[pl.ds(start, BIG), :] = product(start)
         send(x.at[pl.ds(start, BIG)], core_in.at[i], core_send, core_recv.at[i], sibling)
 
+    def pair_of(core, first, half, pair):
+        return pl.multiple_of(core * HALF + first * BIG + half * HALF_BIG + pair * PAIR, PAIR)
+
+    def group_of(core, first, half, second):
+        return pl.multiple_of(core * HALF + first * BIG + half * HALF_BIG + second * GROUP, GROUP)
+
+    def flipped(place, flip):
+        return (place // 2 + flip // 2) % 2 * 2 + (place + flip) % 2
+
+    def to_axis(i, half):
+        for flip in (3, 2, 1, 0):
+            rows = pl.ds(group_of(ci, (a + FAR[i]) % 4, half, flipped(b, flip)), GROUP)
+            send(x.at[rows], a_in.at[i, half, flip], a_send, a_recv.at[i, half, flip], a_peer(FAR[i]))
+
     def for_axis(i):
         start = pl.multiple_of(ci * HALF + ((a + FAR[i]) % 4) * BIG, BIG)
         value = product(start)
         land(core_in.at[i], core_recv.at[i])
         x[pl.ds(start, BIG), :] = value + core_in[i]
         if FAR[i]:
-            for j, kb in enumerate(FAR):
-                rows = pl.ds(pl.multiple_of(start + ((b + kb) % 4) * MID, MID), MID)
-                send(x.at[rows], a_in.at[i, j], a_send, a_recv.at[i, j], a_peer(FAR[i]))
+            to_axis(i, 0)
 
     gram[...] = lax.dot_general(span[...], span[...], (((0,), (0,)), ((), ())),
                                 precision=lax.Precision.HIGHEST, preferred_element_type=jnp.float32)
@@ -215,6 +235,8 @@
     for_axis(1)
     for_sibling(3)
     for_axis(2)
+    for i in range(3):
+        to_axis(i, 1)
     for_axis(3)
     row = lax.broadcasted_iota(jnp.int32, (RANK, RANK), 0)
     lane = lax.broadcasted_iota(jnp.int32, (RANK, RANK), 1)
@@ -230,59 +252,66 @@
             return 0
         lax.fori_loop(first, last, one, 0)
 
-    own = pl.multiple_of(ci * HALF + a * BIG, BIG)
-    for j, kb in enumerate(FAR):
-        block = pl.multiple_of(own + ((b + kb) % 4) * MID, MID)
-        rows = pl.ds(block, MID)
+    def to_owners(half, flip):
+        block = group_of(ci, a, half, flipped(b, flip))
+        rows = pl.ds(block, GROUP)
         for i in range(3):
-            land(a_in.at[i, j], a_recv.at[i, j])
-        x[rows, :] = x[rows, :] + a_in[0, j] + a_in[1, j] + a_in[2, j]
+            land(a_in.at[i, half, flip], a_recv.at[i, half, flip])
+        x[rows, :] = x[rows, :] + a_in[0, half, flip] + a_in[1, half, flip] + a_in[2, half, flip]
         for kz in FAR_Z:
-            if kb or kz:
-                piece = pl.ds(pl.multiple_of(block + ((zi + kz) % ZS) * SMALL, SMALL), SMALL)
-                slot = ZS * j + kz - (1 if kb == 0 else 0)
-                send(x.at[piece], z_in.at[slot], z_send, z_recv, bz_peer(kb, kz))
-        if j == 0:
-            land(gram_x, gram_recv.at[1])
-            land(gram_x, gram_send.at[1])
-            gram[mine, :] = gram[mine, :] + gram_x[0] + gram_x[1] + gram_x[2]
-            send(gram.at[mine], gram_back, gram_send.at[2], gram_recv.at[2], sibling)
-            lower[mine, :] = gram[mine, :]
-        if j == 1:
-            land(gram_back, gram_recv.at[2])
-            lower[other, :] = gram_back[...]
-            eliminate(0, 1)
-        if j == 2:
-            eliminate(1, 3)
+            if flip or kz:
+                piece = pl.ds(pl.multiple_of(block + (zi + kz) % ZS * SMALL, SMALL), SMALL)
+                slot = ZS * (3 - flip) + kz - (1 if flip == 0 else 0)
+                send(x.at[piece], z_in.at[half, slot], z_send, z_recv.at[half], bz_peer(flip, kz))
+
+    to_owners(0, 3)
+    to_owners(0, 2)
+    land(gram_x, gram_recv.at[1])
+    land(gram_x, gram_send.at[1])
+    gram[mine, :] = gram[mine, :] + gram_x[0] + gram_x[1] + gram_x[2]
+    send(gram.at[mine], gram_back, gram_send.at[2], gram_recv.at[2], sibling)
+    lower[mine, :] = gram[mine, :]
+    to_owners(0, 1)
+    to_owners(0, 0)
+    land(gram_back, gram_recv.at[2])
+    lower[other, :] = gram_back[...]
+    eliminate(0, 1)
+    to_owners(1, 3)
+    eliminate(1, 2)
+    to_owners(1, 2)
+    eliminate(2, 3)
+    to_owners(1, 1)
     eliminate(3, 4)
+    to_owners(1, 0)
     eliminate(4, 8)
     eliminate(8, 12)
     eliminate(12, 16)
+
+    def spread_rows(half):
+        rows = pl.ds(pl.multiple_of(group_of(ci, a, half, b) + zi * SMALL, SMALL), SMALL)
+        land(z_in.at[half], z_recv.at[half])
+        total = x[rows, :]
+        for k in range(4 * ZS - 1):
+            total = total + z_in[half, k]
+        n_ref[rows, :] = lax.dot_general(total * (1.0 / DP), inverse[...], (((1,), (1,)), ((), ())),
+                                         precision=lax.Precision.HIGHEST, preferred_element_type=jnp.float32)
+        for flip in range(4):
+            for kz in FAR_Z:
+                if flip or kz:
+                    send(n_ref.at[rows], n_ref.at[rows], gz_send, gz_recv.at[half, flip], bz_peer(flip, kz))
+
+    spread_rows(0)
     span_in_basis = lax.dot_general(span[...], inverse[...], (((1,), (1,)), ((), ())),
                                     precision=lax.Precision.HIGHEST, preferred_element_type=jnp.float32)
     high, low = split(span_in_basis)
     o2[:, :RANK] = high
     o2[:, RANK:] = low
-    last = pl.ds(pl.multiple_of(own + b * MID + zi * SMALL, SMALL), SMALL)
-    land(z_in, z_recv)
-    total = x[last, :]
-    for k in range(4 * ZS - 1):
-        total = total + z_in[k]
-
-    n_ref[last, :] = lax.dot_general(total * (1.0 / DP), inverse[...], (((1,), (1,)), ((), ())),
-                                     precision=lax.Precision.HIGHEST, preferred_element_type=jnp.float32)
-    for j, kb in enumerate(NEAR):
-        for kz in FAR_Z:
-            if kb or kz:
-                send(n_ref.at[last], n_ref.at[last], gz_send, gz_recv.at[j], bz_peer(kb, kz))
-
-    def block_of(core, first, second):
-        return pl.multiple_of(core * HALF + first * BIG + second * MID, MID)
-
-    def residual(start):
+    spread_rows(1)
+
+    def residual(start, width):
         @pl.when(start < D)
         def _():
-            cols = pl.ds(start, MID)
+            cols = pl.ds(start, width)
             high, low = split(n_ref[cols, :])
             update = (lax.dot_general(o2[...], jnp.concatenate([high, high], 1), (((1,), (1,)), ((), ())),
                                       preferred_element_type=jnp.float32)
@@ -293,34 +322,72 @@
                              + gm[192 * q + 96:192 * q + 192, cols].astype(jnp.float32))
                 new_ref[96 * q:96 * (q + 1), cols] = (corrected - update[96 * q:96 * (q + 1)]).astype(jnp.bfloat16)
 
-    arrivals = [(i, j) for i in (3,) for j in range(4)] + [(i, j) for j in range(4) for i in range(3)]
-
-    def take_own(i, j):
-        if i == 3:
-            start = block_of(ci, a, (b - NEAR[j] + 4) % 4)
-            here = pl.ds(start, MID)
-            land(n_ref.at[pl.ds(0, (ZS - 1) * SMALL if NEAR[j] == 0 else MID)], gz_recv.at[j])
-            for r in range(3):
-                send(n_ref.at[here], n_ref.at[here], ga_send, ga_recv.at[r, j], a_peer(FAR[r]))
+    def from_owners(half, flip):
+        rows = pl.ds(group_of(ci, a, half, flipped(b, flip)), GROUP)
+        land(n_ref.at[pl.ds(0, GROUP - (SMALL if flip == 0 else 0))], gz_recv.at[half, flip])
+        for r in range(3):
+            send(n_ref.at[rows], n_ref.at[rows], ga_send, ga_recv.at[r, half, flip], a_peer(FAR[r]))
+        send(n_ref.at[rows], n_ref.at[rows], gc_send, gc_recv.at[3, half, flip], sibling)
+
+    def from_axis(half, flip):
+        for i in (1, 2, 0):
+            rows = pl.ds(group_of(ci, (a - FAR[i] + 4) % 4, half, flipped(b, flip)), GROUP)
+            land(n_ref.at[rows], ga_recv.at[i, half, flip])
+            send(n_ref.at[rows], n_ref.at[rows], gc_send, gc_recv.at[i, half, flip], sibling)
+
+    def from_sibling(i, half, flips):
+        for flip in flips:
+            land(n_ref.at[pl.ds(0, GROUP)], gc_recv.at[i, half, flip])
+
+    DISTANCES = FAR[:3] + (0,)
+
+    def own_columns(i, half, p=None):
+        if p is None:
+            residual(pl.multiple_of(pair_of(ci, (a - DISTANCES[i] + 4) % 4, half, 0), HALF_BIG), HALF_BIG)
         else:
-            start = block_of(ci, (a - FAR[i] + 4) % 4, (b - NEAR[j] + 4) % 4)
-            here = pl.ds(start, MID)
-            land(n_ref.at[here], ga_recv.at[i, j])
-        send(n_ref.at[here], n_ref.at[here], gc_send, gc_recv.at[i, j], sibling)
-        return start
-
-    def take_sibling(i, j):
-        start = block_of(1 - ci, (b - FAR[i] + 4) % 4, (a - NEAR[j] + 4) % 4)
-        land(n_ref.at[pl.ds(start, MID)], gc_recv.at[i, j])
-        residual(start)
-
-    for n, (i, j) in enumerate(arrivals):
-        start = take_own(i, j)
-        residual(start)
-        if n >= 4:
-            take_sibling(*arrivals[n - 4])
-    for i, j in arrivals[-4:]:
-        take_sibling(i, j)
+            residual(pair_of(ci, (a - DISTANCES[i] + 4) % 4, half, (b // 2 + p) % 2), PAIR)
+
+    def sibling_columns(i, half, p=None):
+        if p is None:
+            residual(pl.multiple_of(pair_of(1 - ci, (b - DISTANCES[i] + 4) % 4, half, 0), HALF_BIG), HALF_BIG)
+        else:
+            residual(pair_of(1 - ci, (b - DISTANCES[i] + 4) % 4, half, (a // 2 + p) % 2), PAIR)
+
+    from_owners(0, 0)
+    from_owners(0, 1)
+    own_columns(3, 0, 0)
+    from_owners(1, 0)
+    from_owners(0, 2)
+    from_owners(0, 3)
+    own_columns(3, 0, 1)
+    from_axis(0, 0)
+    from_owners(1, 1)
+    own_columns(3, 1, 0)
+    from_axis(0, 1)
+    from_owners(1, 2)
+    from_axis(1, 0)
+    from_owners(1, 3)
+    own_columns(3, 1, 1)
+    from_axis(0, 2)
+    from_axis(0, 3)
+    for i in range(3):
+        own_columns(i, 0)
+    from_axis(1, 1)
+    for i in (3, 1, 2, 0):
+        from_sibling(i, 0, range(4))
+        sibling_columns(i, 0)
+    from_axis(1, 2)
+    for i in range(3):
+        own_columns(i, 1, 0)
+    from_axis(1, 3)
+    for i in (3, 1, 2, 0):
+        from_sibling(i, 1, (0, 1))
+        sibling_columns(i, 1, 0)
+    for i in range(3):
+        own_columns(i, 1, 1)
+    for i in (3, 1, 2, 0):
+        from_sibling(i, 1, (2, 3))
+        sibling_columns(i, 1, 1)
 
     land(part_y, party_send)
     land(part_z, part_send)
@@ -341,10 +408,10 @@
     return pl.pallas_call(
         exchange_kernel,
         out_shape=(jax.ShapeDtypeStruct((ROWS, D), bf16), jax.ShapeDtypeStruct((PADDED, RANK), f32)),
-        in_specs=[pl.BlockSpec(memory_space=pltpu.HBM)] * 2 + [pl.BlockSpec(memory_space=pltpu.VMEM)],
+        in_specs=[pl.BlockSpec(memory_space=pltpu.HBM)] * 3,
         out_specs=(pl.BlockSpec(memory_space=pltpu.VMEM), pl.BlockSpec(memory_space=pltpu.VMEM)),
         scratch_shapes=[
-            pltpu.VMEM((2 * ROWS, D), bf16), pltpu.VMEM((PADDED, 2 * ROWS), bf16),
+            pltpu.VMEM((2 * ROWS, D), bf16), pltpu.VMEM((D, RANK), bf16), pltpu.VMEM((PADDED, 2 * ROWS), bf16),
             pltpu.VMEM((DP, PIECE, RANK), f32), pltpu.VMEM((3, ZS, PIECE, RANK), f32),
             pltpu.VMEM((ZS - 1, PIECE, RANK), f32),
             pltpu.VMEM((DP, PIECE, RANK), f32), pltpu.VMEM((ROWS, RANK), f32),
@@ -353,12 +420,11 @@
             pltpu.VMEM((64, RANK), f32), pltpu.VMEM((RANK, RANK), f32), pltpu.VMEM((RANK, RANK), f32),
             pltpu.VMEM((RANK, RANK), f32),
             pltpu.VMEM((PADDED, RANK), f32), pltpu.VMEM((4, BIG, RANK), f32),
-            pltpu.VMEM((3, 4, MID, RANK), f32), pltpu.VMEM((4 * ZS - 1, SMALL, RANK), f32),
-            dma((8,)), dma, dma((3,)), dma, dma, dma, dma, dma((3,)), dma((3,)), dma, dma((4,)), dma, dma((3, 4)), dma, dma,
-            dma, dma((4,)), dma, dma((3, 4)), dma, dma((4, 4)),
+            pltpu.VMEM((3, 2, 4, GROUP, RANK), f32), pltpu.VMEM((2, 4 * ZS - 1, SMALL, RANK), f32),
+            dma((9,)), dma, dma((3,)), dma, dma, dma, dma, dma((3,)), dma((3,)), dma, dma((4,)), dma, dma((3, 2, 4)), dma, dma((2,)),
+            dma, dma((2, 4)), dma, dma((3, 2, 4)), dma, dma((4, 2, 4)),
         ],
         compiler_params=pltpu.CompilerParams(collective_id=0, has_side_effects=True, vmem_limit_bytes=VMEM_BYTES),
-        cost_estimate=pl.CostEstimate(flops=4 * 10 ** 9, bytes_accessed=10 ** 7, transcendentals=0),
         name="exchange",
     )(g, m, f)
 
@@ -388,7 +454,7 @@
 
 
 def per_device(gradient, memory, old_factor):
-    new_memory, new_factor = store(*exchange(gradient[0], memory[0], old_factor))
+    new_memory, new_factor = store(*exchange(gradient[0], memory[0], pltpu.with_memory_space_constraint(old_factor, pltpu.HBM)))
     return (new_memory[None], new_factor)
 
 

time: 65.9 us -> 63.8 us (0.968)
  local copies, waits for them, and re-layouts: 1.21 us -> 0 us
  Pallas kernels: 63.9 us -> 63 us
    unnamed x2 -> x0, local copies, waits for them, and re-layouts: 1.21 us -> none
    pallas_call x1, Pallas kernels: 61.6 us -> 60.7 us  [exchange(): pl.pallas_call(exchange_kernel, out_shape=(jax.ShapeDtypeStruct((ROWS, D)...]
where the time goes in v4:
time: 63.8 us; the launch traced here: 63.7 us
  Pallas kernels  63 us (99%)
  between operations  0.64 us (1%)
    pallas_call x1, Pallas kernels, exchange(): pl.pallas_call(exchange_kernel, out_shape=(jax.ShapeDtypeStruct((ROWS, D)...  60.7 us
    pallas_call x1, Pallas kernels, store(): pl.pallas_call(store_kernel, out_shape=(jax.ShapeDtypeStruct((ROWS, D), j...  2.36 us

profile of v4, /device:TPU:1, one launch (start us, length us, event | category | flops | bytes accessed | tf_op | source)
XLA Modules:
  0.0 63.7 jit_solution(2155300046690402612)
XLA Ops:
  0.6 60.7 %exchange.1 = (bf16[384,3968]{1,0:T(8,128)(2,1)S(1)}, f32[4096,128]{1,0:T(8,128)S(1)}) custom-call(bf16[384,3968]{1,0:T(8,128)(2,1)} %bitcast.3, bf16[384,3968]{1,0:T(8,128)(2,1)} %bitcast.4, bf16[3968,128]{1,0:T(8,128)(2,1)} %f_hbm.1), custom_call_target="tpu_custom_call" | custom-call | tf_op jit(solution)/shard_map/exchange/pallas_call | solution.py:408
  61.3 2.4 %store.1 = (bf16[384,3968]{1,0:T(8,128)(2,1)}, f32[3968,128]{1,0:T(8,128)}) custom-call(bf16[384,3968]{1,0:T(8,128)(2,1)S(1)} %get-tuple-element.6.new_ref, f32[4096,128]{1,0:T(8,128)S(1)} %get-tuple-element.7.n_ref), custom_call_target="tpu_custom_call" | custom-call | tf_op jit(solution)/shard_map/store/pallas_call | solution.py:445

commit v5 on v4

--- a/solution.py
+++ b/solution.py
@@ -341,33 +341,38 @@
 
     DISTANCES = FAR[:3] + (0,)
 
-    def own_columns(i, half, p=None):
-        if p is None:
-            residual(pl.multiple_of(pair_of(ci, (a - DISTANCES[i] + 4) % 4, half, 0), HALF_BIG), HALF_BIG)
+    def whole(core, first, half):
+        start = pl.multiple_of(pair_of(core, first, half, 0), HALF_BIG)
+        if half == 0:
+            residual(start, HALF_BIG)
         else:
-            residual(pair_of(ci, (a - DISTANCES[i] + 4) % 4, half, (b // 2 + p) % 2), PAIR)
-
-    def sibling_columns(i, half, p=None):
-        if p is None:
-            residual(pl.multiple_of(pair_of(1 - ci, (b - DISTANCES[i] + 4) % 4, half, 0), HALF_BIG), HALF_BIG)
-        else:
-            residual(pair_of(1 - ci, (b - DISTANCES[i] + 4) % 4, half, (a // 2 + p) % 2), PAIR)
+            @pl.when(start + HALF_BIG <= D)
+            def _():
+                residual(start, HALF_BIG)
+
+            @pl.when(start + HALF_BIG > D)
+            def _():
+                residual(pl.multiple_of(start, PAIR), PAIR)
+
+    def own_columns(i, half):
+        whole(ci, (a - DISTANCES[i] + 4) % 4, half)
+
+    def sibling_columns(i, half):
+        whole(1 - ci, (b - DISTANCES[i] + 4) % 4, half)
 
     from_owners(0, 0)
     from_owners(0, 1)
-    own_columns(3, 0, 0)
     from_owners(1, 0)
     from_owners(0, 2)
     from_owners(0, 3)
-    own_columns(3, 0, 1)
     from_axis(0, 0)
+    own_columns(3, 0)
     from_owners(1, 1)
-    own_columns(3, 1, 0)
     from_axis(0, 1)
     from_owners(1, 2)
     from_axis(1, 0)
     from_owners(1, 3)
-    own_columns(3, 1, 1)
+    own_columns(3, 1)
     from_axis(0, 2)
     from_axis(0, 3)
     for i in range(3):
@@ -377,17 +382,14 @@
         from_sibling(i, 0, range(4))
         sibling_columns(i, 0)
     from_axis(1, 2)
+    from_axis(1, 3)
+    from_sibling(3, 1, range(4))
+    sibling_columns(3, 1)
     for i in range(3):
-        own_columns(i, 1, 0)
-    from_axis(1, 3)
-    for i in (3, 1, 2, 0):
-        from_sibling(i, 1, (0, 1))
-        sibling_columns(i, 1, 0)
-    for i in range(3):
-        own_columns(i, 1, 1)
-    for i in (3, 1, 2, 0):
-        from_sibling(i, 1, (2, 3))
-        sibling_columns(i, 1, 1)
+        own_columns(i, 1)
+    for i in (1, 2, 0):
+        from_sibling(i, 1, range(4))
+        sibling_columns(i, 1)
 
     land(part_y, party_send)
     land(part_z, part_send)

time: 63.8 us -> 63.2 us (level)
  no operation moved by 1% of the time
where the time goes in v5:
time: 63.2 us; the launch traced here: 63.1 us
  Pallas kernels  62.4 us (99%)
  between operations  0.64 us (1%)
    pallas_call x1, Pallas kernels, exchange(): pl.pallas_call(exchange_kernel, out_shape=(jax.ShapeDtypeStruct((ROWS, D)...  60.1 us
    pallas_call x1, Pallas kernels, store(): pl.pallas_call(store_kernel, out_shape=(jax.ShapeDtypeStruct((ROWS, D), j...  2.36 us

profile of v5, /device:TPU:1, one launch (start us, length us, event | category | flops | bytes accessed | tf_op | source)
XLA Modules:
  0.0 63.1 jit_solution(17999049608954170777)
XLA Ops:
  0.6 60.1 %exchange.1 = (bf16[384,3968]{1,0:T(8,128)(2,1)S(1)}, f32[4096,128]{1,0:T(8,128)S(1)}) custom-call(bf16[384,3968]{1,0:T(8,128)(2,1)} %bitcast.3, bf16[384,3968]{1,0:T(8,128)(2,1)} %bitcast.4, bf16[3968,128]{1,0:T(8,128)(2,1)} %f_hbm.1), custom_call_target="tpu_custom_call" | custom-call | tf_op jit(solution)/shard_map/exchange/pallas_call | solution.py:410
  60.7 2.4 %store.1 = (bf16[384,3968]{1,0:T(8,128)(2,1)}, f32[3968,128]{1,0:T(8,128)}) custom-call(bf16[384,3968]{1,0:T(8,128)(2,1)S(1)} %get-tuple-element.6.new_ref, f32[4096,128]{1,0:T(8,128)S(1)} %get-tuple-element.7.n_ref), custom_call_target="tpu_custom_call" | custom-call | tf_op jit(solution)/shard_map/store/pallas_call | solution.py:447

commit v6 on v5

--- a/solution.py
+++ b/solution.py
@@ -190,12 +190,19 @@
     mine = pl.ds(pl.multiple_of(ci * 64, 64), 64)
     other = pl.ds(pl.multiple_of((1 - ci) * 64, 64), 64)
 
-    def product(start):
-        both = jnp.dot(gmt[pl.ds(start, BIG), :], span2[...], preferred_element_type=jnp.float32)
+    def product(start, size=BIG):
+        both = jnp.dot(gmt[pl.ds(start, size), :], span2[...], preferred_element_type=jnp.float32)
         return both[:, :RANK] + both[:, RANK:]
 
     def for_sibling(i):
         start = pl.multiple_of((1 - ci) * HALF + ((b + FAR[i]) % 4) * BIG, BIG)
+        if i == 0:
+            for half in (0, 1):
+                rows = pl.ds(pl.multiple_of(start + half * HALF_BIG, HALF_BIG), HALF_BIG)
+                x[rows, :] = product(rows.start, HALF_BIG)
+                send(x.at[rows], core_in.at[0, pl.ds(half * HALF_BIG, HALF_BIG)], core_send, core_recv.at[4 * half],
+                     sibling)
+            return
         x[pl.ds(start, BIG), :] = product(start)
         send(x.at[pl.ds(start, BIG)], core_in.at[i], core_send, core_recv.at[i], sibling)
 
@@ -215,6 +222,16 @@
 
     def for_axis(i):
         start = pl.multiple_of(ci * HALF + ((a + FAR[i]) % 4) * BIG, BIG)
+        if i == 0:
+            for half in (0, 1):
+                rows = pl.ds(pl.multiple_of(start + half * HALF_BIG, HALF_BIG), HALF_BIG)
+                part_in = pl.ds(half * HALF_BIG, HALF_BIG)
+                value = product(rows.start, HALF_BIG)
+                land(core_in.at[0, part_in], core_recv.at[4 * half])
+                x[rows, :] = value + core_in[0, part_in, :]
+                if half == 0:
+                    to_axis(i, 0)
+            return
         value = product(start)
         land(core_in.at[i], core_recv.at[i])
         x[pl.ds(start, BIG), :] = value + core_in[i]
@@ -423,7 +440,7 @@
             pltpu.VMEM((RANK, RANK), f32),
             pltpu.VMEM((PADDED, RANK), f32), pltpu.VMEM((4, BIG, RANK), f32),
             pltpu.VMEM((3, 2, 4, GROUP, RANK), f32), pltpu.VMEM((2, 4 * ZS - 1, SMALL, RANK), f32),
-            dma((9,)), dma, dma((3,)), dma, dma, dma, dma, dma((3,)), dma((3,)), dma, dma((4,)), dma, dma((3, 2, 4)), dma, dma((2,)),
+            dma((9,)), dma, dma((3,)), dma, dma, dma, dma, dma((3,)), dma((3,)), dma, dma((5,)), dma, dma((3, 2, 4)), dma, dma((2,)),
             dma, dma((2, 4)), dma, dma((3, 2, 4)), dma, dma((4, 2, 4)),
         ],
         compiler_params=pltpu.CompilerParams(collective_id=0, has_side_effects=True, vmem_limit_bytes=VMEM_BYTES),

time: 63.2 us -> 63.2 us (level)
  no operation moved by 1% of the time
where the time goes in v6:
time: 63.2 us; the launch traced here: 63.1 us
  Pallas kernels  62.5 us (99%)
  between operations  0.64 us (1%)
    pallas_call x1, Pallas kernels, exchange(): pl.pallas_call(exchange_kernel, out_shape=(jax.ShapeDtypeStruct((ROWS, D)...  60.1 us
    pallas_call x1, Pallas kernels, store(): pl.pallas_call(store_kernel, out_shape=(jax.ShapeDtypeStruct((ROWS, D), j...  2.36 us

profile of v6, /device:TPU:1, one launch (start us, length us, event | category | flops | bytes accessed | tf_op | source)
XLA Modules:
  0.0 63.1 jit_solution(2974393618280650931)
XLA Ops:
  0.6 60.1 %exchange.1 = (bf16[384,3968]{1,0:T(8,128)(2,1)S(1)}, f32[4096,128]{1,0:T(8,128)S(1)}) custom-call(bf16[384,3968]{1,0:T(8,128)(2,1)} %bitcast.3, bf16[384,3968]{1,0:T(8,128)(2,1)} %bitcast.4, bf16[3968,128]{1,0:T(8,128)(2,1)} %f_hbm.1), custom_call_target="tpu_custom_call" | custom-call | tf_op jit(solution)/shard_map/exchange/pallas_call | solution.py:427
  60.7 2.4 %store.1 = (bf16[384,3968]{1,0:T(8,128)(2,1)}, f32[3968,128]{1,0:T(8,128)}) custom-call(bf16[384,3968]{1,0:T(8,128)(2,1)S(1)} %get-tuple-element.6.new_ref, f32[4096,128]{1,0:T(8,128)S(1)} %get-tuple-element.7.n_ref), custom_call_target="tpu_custom_call" | custom-call | tf_op jit(solution)/shard_map/store/pallas_call | solution.py:464
